TPU v7x, 128 devices: a whole 4x4x4 slice. The times are simulated.
128 devices in a mesh: ma: 64 (over x, y, z_lo, core), ha: 2 (over z_hi).
Axes of the slice: x: 4, y: 4, z: 4 (z_hi: 2, z_lo: 2; z = z_hi * 2 + z_lo), core: 2. Of those that a mesh axis runs over, the one named last changes fastest.
Arguments:
- coefficients: bfloat16 [2, 1024, 10, 2, 1024], P('ha', 'ma'), may hold values from -2 to 2
- section_factors: bfloat16 [2, 1024, 64, 1024], P('ha', 'ma'), may hold values from -0.75 to 0.75
- level_factors: bfloat16 [2, 2, 1024, 64, 2048], P('ha', None, 'ma'), may hold values from -0.5 to 0.5
- partners: int32 [2, 16], replicated, may hold values from 0 to 15, as said below
- wave_ids: int32 [1024], replicated, may hold values from 0 to 1023, as said below
Outputs:
- grid: bfloat16 [2, 1024, 10, 4096], P(None, ('ma', 'ha'))
- slope: bfloat16 [2, 1024, 10, 4096], P(None, ('ma', 'ha'))
Inputs may be any that keep to these rules, and one draw needn't show every extreme that they name: `partners`: row l pairs the 16 blocks: no block is its own partner, and the partner of a block's partner is the block itself. `wave_ids`: A permutation of the wavenumbers; slots 2 q and 2 q + 1 hold a wavenumber m and 1023 - m.
All inputs are finite; a program needn't handle non-finite values.
Results may differ from a plain program's by a relative error of at most 0.0075.
Values may be sent and summed in bfloat16 or wider, within the bound.
A program may use at most 192 MiB of HBM per device.

v0:
```python
import math

import jax
import jax.numpy as jnp
from jax import lax
from jax.sharding import PartitionSpec as P

NLON = 4096
K = 64


def body(coefficients, section_factors, level_factors, partners, wave_ids):
    parity = lax.axis_index("ha")
    band = lax.axis_index("ma")
    n_ma = lax.axis_size("ma")
    m_dev = coefficients.shape[1]
    nfield = coefficients.shape[2]
    lath = coefficients.shape[4]
    rank = K
    nblock = lath // rank
    total = m_dev * n_ma
    rows = lath // (2 * n_ma)
    mine = lax.dynamic_slice_in_dim(wave_ids, band * m_dev, m_dev, 0)
    degree = mine[:, None] + 2 * jnp.arange(lath, dtype=jnp.int32)[None, :] + parity
    keep = (degree <= total - 1).astype(jnp.bfloat16)
    masked = coefficients[0] * keep[:, None, None, :]
    blocks = masked.reshape(m_dev, nfield, 2, nblock, rank)
    section_blocks = section_factors[0].reshape(m_dev, rank, nblock, rank)
    state = jnp.einsum(
        "mibj,mfrbj->mfrbi", section_blocks, blocks, preferred_element_type=jnp.float32
    ).astype(jnp.bfloat16)
    block_ids = jnp.arange(nblock, dtype=jnp.int32)
    for level in range(level_factors.shape[1]):
        onehot = (partners[level][:, None] == block_ids[None, :]).astype(jnp.bfloat16)
        across = jnp.einsum(
            "bc,mfrcj->mfrbj", onehot, state, preferred_element_type=jnp.float32
        ).astype(jnp.bfloat16)
        factors = level_factors[0, level].reshape(m_dev, rank, nblock, 2, rank)
        summed = jnp.einsum(
            "mibj,mfrbj->mfrbi", factors[:, :, :, 0], state, preferred_element_type=jnp.float32
        )
        summed = summed + jnp.einsum(
            "mibj,mfrbj->mfrbi", factors[:, :, :, 1], across, preferred_element_type=jnp.float32
        )
        state = summed.astype(jnp.bfloat16)
    partial_value = state.reshape(1, m_dev, nfield, 2, lath)
    banded = lax.all_to_all(partial_value, "ma", split_axis=4, concat_axis=0, tiled=True)
    paired = lax.all_to_all(banded[None], "ha", split_axis=5, concat_axis=0, tiled=True)
    evens = paired[0]
    odds = paired[1]
    even_part = evens.astype(jnp.float32)
    odd_part = odds.astype(jnp.float32)
    spectra = jnp.stack([even_part + odd_part, even_part - odd_part]).astype(jnp.bfloat16)
    real_left = jnp.transpose(spectra[:, :, :, :, 0], (0, 4, 3, 1, 2)).reshape(
        2 * rows * nfield, total
    )
    imag_left = jnp.transpose(spectra[:, :, :, :, 1], (0, 4, 3, 1, 2)).reshape(
        2 * rows * nfield, total
    )
    waves = wave_ids.astype(jnp.float32)
    weight = jnp.where(wave_ids > 0, 2.0, 1.0).astype(jnp.float32)[:, None]
    scaled = weight * (waves / total)[:, None]
    width = min(512, NLON)
    grid_parts = []
    slope_parts = []
    for start in range(0, NLON, width):
        lon = start + jnp.arange(width, dtype=jnp.int32)
        phase = (wave_ids[:, None] * lon[None, :] % NLON).astype(jnp.float32) * (
            2.0 * math.pi / NLON
        )
        cosine = jnp.cos(phase)
        sine = jnp.sin(phase)
        cos_value = (weight * cosine).astype(jnp.bfloat16)
        sin_value = (-weight * sine).astype(jnp.bfloat16)
        sin_turned = (-scaled * sine).astype(jnp.bfloat16)
        cos_turned = (-scaled * cosine).astype(jnp.bfloat16)
        grid_block = jnp.dot(real_left, cos_value, preferred_element_type=jnp.float32) + jnp.dot(
            imag_left, sin_value, preferred_element_type=jnp.float32
        )
        slope_block = jnp.dot(real_left, sin_turned, preferred_element_type=jnp.float32) + jnp.dot(
            imag_left, cos_turned, preferred_element_type=jnp.float32
        )
        grid_parts.append(grid_block.astype(jnp.bfloat16))
        slope_parts.append(slope_block.astype(jnp.bfloat16))
    grid = jnp.concatenate(grid_parts, axis=1).reshape(2, rows, nfield, NLON)
    slope = jnp.concatenate(slope_parts, axis=1).reshape(2, rows, nfield, NLON)
    return (grid, slope)


def solution(mesh):
    in_specs = (
        P("ha", "ma", None, None, None),
        P("ha", "ma", None, None),
        P("ha", None, "ma", None, None),
        P(),
        P(),
    )
    out_specs = (P(None, ("ma", "ha"), None, None), P(None, ("ma", "ha"), None, None))
    return jax.shard_map(body, mesh=mesh, in_specs=in_specs, out_specs=out_specs, check_vma=False)
```

profile of v0, /device:TPU:1, one launch (start us, length us, event | category | flops | bytes accessed | tf_op | source)
XLA Modules:
  0.0 488.1 jit_solution(2357576120283319482)
XLA Ops:
  14.0 15.9 %reshape_squeeze.10 = bf16[16,64,16,2,64]{4,3,2,1,0:T(2,128)(2,1)} reshape(bf16[1,1,16,64,2048]{4,3,2,1,0:T(8,128)(2,1)} %get-tuple-element.12) | data formatting | bytes 8388608 | tf_op jit(solution)/shard_map/reshape;squeeze | solution.py:38
  29.9 17.8 %fusion.316 = (bf16[16,64,16,1,64]{4,3,2,1,0:T(2,128)(2,1)}, bf16[16,64,16,1,64]{4,3,2,1,0:T(2,128)(2,1)}) fusion(bf16[16,64,16,2,64]{4,3,2,1,0:T(2,128)(2,1)} %reshape_squeeze.10), kind=kLoop, calls=%fused_computation.397 | loop fusion | bytes 8388608 | tf_op jit(solution)/shard_map/slice | solution.py:40
  47.7 15.9 %reshape_squeeze.11 = bf16[16,64,16,2,64]{4,3,2,1,0:T(2,128)(2,1)} reshape(bf16[1,1,16,64,2048]{4,3,2,1,0:T(8,128)(2,1)} %get-tuple-element.13) | data formatting | bytes 8388608 | tf_op jit(solution)/shard_map/reshape;squeeze | solution.py:38
  63.5 18.2 %fusion.315 = (bf16[16,64,16,1,64]{4,3,2,1,0:T(2,128)(2,1)}, bf16[16,64,16,1,64]{4,3,2,1,0:T(2,128)(2,1)}) fusion(bf16[16,64,16,2,64]{4,3,2,1,0:T(2,128)(2,1)} %reshape_squeeze.11), kind=kLoop, calls=%fused_computation.396 | loop fusion | bytes 8388608 | tf_op jit(solution)/shard_map/slice | solution.py:40
  116.7 15.6 %reshape.149 = bf16[64,2,2560]{2,1,0:T(2,128)(2,1)} reshape(bf16[1024,1,10,2,16]{4,3,2,1,0:T(2,128)(2,1)} %bitcast.129) | data formatting | bytes 1310720
  132.4 10.3 %all-to-all-start = ((bf16[64,2,2560]{2,1,0:T(2,128)(2,1)}), bf16[64,2,2560]{2,1,0:T(2,128)(2,1)S(1)}, u32[]{:S(2)}, u32[]{:S(2)}) async-start(bf16[64,2,2560]{2,1,0:T(2,128)(2,1)} %reshape.149), calls=%async_computation | async-start | bytes 1310720 | tf_op jit(solution)/shard_map/all_to_all | solution.py:47
  142.8 13.8 %all-to-all-done = bf16[64,2,2560]{2,1,0:T(2,128)(2,1)S(1)} async-done(((bf16[64,2,2560]{2,1,0:T(2,128)(2,1)}), bf16[64,2,2560]{2,1,0:T(2,128)(2,1)S(1)}, u32[]{:S(2)}, u32[]{:S(2)}) %all-to-all-start) | async-done | bytes 655392 | tf_op jit(solution)/shard_map/all_to_all | solution.py:47
  161.6 9.7 %copy.56 = bf16[1,16,10,2,64,16]{4,1,3,2,5,0:T(8,128)(2,1)S(1)} copy(bf16[1,16,10,2,64,16]{1,3,2,5,4,0:T(2,128)(2,1)} %bitcast.130) | data formatting | bytes 1310720 | tf_op jit(solution)/shard_map/broadcast_in_dim | solution.py:48
  177.9 10.3 %all-to-all-done.1 = bf16[2,2,81920]{2,1,0:T(2,128)(2,1)S(1)} async-done(((bf16[2,2,81920]{2,1,0:T(2,128)(2,1)}), bf16[2,2,81920]{2,1,0:T(2,128)(2,1)S(1)}, u32[]{:S(2)}, u32[]{:S(2)}) %all-to-all-start.1) | async-done | bytes 655392 | tf_op jit(solution)/shard_map/all_to_all | solution.py:48
  200.0 9.9 %fusion.85 = f32[160,512]{1,0:T(8,128)} fusion(bf16[160,1024]{1,0:T(8,128)(2,1)} %reshape.138, f32[1024]{0:T(1024)S(1)} %get-tuple-element.18, s32[1024]{0:T(1024)S(1)} %copy-done.6), kind=kOutput, calls=%fused_computation.184 | convolution fusion | flops 176160768 | bytes 663552 | tf_op jit(solution)/shard_map/dot_general | solution.py:80
  209.9 8.9 %fusion.86 = f32[160,512]{1,0:T(8,128)} fusion(bf16[160,1024]{1,0:T(8,128)(2,1)S(1)} %copy-done.5, f32[1024]{0:T(1024)S(1)} %get-tuple-element.18, s32[512]{0:T(512)S(1)} %iota_add_fusion.6, s32[1024]{0:T(1024)S(1)} %copy-done.6), kind=kOutput, calls=%fused_computation.185 | convolution fusion | flops 176160768 | bytes 665600 | tf_op jit(solution)/shard_map/dot_general | solution.py:80
  218.8 8.9 %fusion.77 = f32[160,512]{1,0:T(8,128)} fusion(bf16[160,1024]{1,0:T(8,128)(2,1)S(1)} %copy-done.5, s32[1024]{0:T(1024)S(1)} %copy-done.6, f32[1024]{0:T(1024)S(1)} %get-tuple-element.20), kind=kOutput, calls=%fused_computation.176 | convolution fusion | flops 176160768 | bytes 663552 | tf_op jit(solution)/shard_map/dot_general | solution.py:77
  227.7 8.7 %fusion.78 = f32[160,512]{1,0:T(8,128)} fusion(bf16[160,1024]{1,0:T(8,128)(2,1)S(1)} %copy-done.5, s32[512]{0:T(512)S(1)} %iota_add_fusion.6, s32[1024]{0:T(1024)S(1)} %copy-done.6, f32[1024]{0:T(1024)S(1)} %get-tuple-element.20), kind=kOutput, calls=%fused_computation.177 | convolution fusion | flops 176160768 | bytes 665600 | tf_op jit(solution)/shard_map/dot_general | solution.py:77
  236.4 9.2 %fusion.87 = f32[160,512]{1,0:T(8,128)} fusion(bf16[160,1024]{1,0:T(8,128)(2,1)S(1)} %copy-done.5, f32[1024]{0:T(1024)S(1)} %get-tuple-element.18, s32[512]{0:T(512)S(1)} %iota_add_fusion.5, s32[1024]{0:T(1024)S(1)} %copy-done.6), kind=kOutput, calls=%fused_computation.186 | convolution fusion | flops 176160768 | bytes 665600 | tf_op jit(solution)/shard_map/dot_general | solution.py:80
  245.6 8.9 %fusion.79 = f32[160,512]{1,0:T(8,128)} fusion(bf16[160,1024]{1,0:T(8,128)(2,1)S(1)} %copy-done.5, s32[512]{0:T(512)S(1)} %iota_add_fusion.5, s32[1024]{0:T(1024)S(1)} %copy-done.6, f32[1024]{0:T(1024)S(1)} %get-tuple-element.20), kind=kOutput, calls=%fused_computation.178 | convolution fusion | flops 176160768 | bytes 665600 | tf_op jit(solution)/shard_map/dot_general | solution.py:77
  254.4 8.7 %fusion.88 = f32[160,512]{1,0:T(8,128)} fusion(bf16[160,1024]{1,0:T(8,128)(2,1)S(1)} %copy-done.5, f32[1024]{0:T(1024)S(1)} %get-tuple-element.18, s32[512]{0:T(512)S(1)} %iota_add_fusion.4, s32[1024]{0:T(1024)S(1)} %copy-done.6), kind=kOutput, calls=%fused_computation.187 | convolution fusion | flops 176160768 | bytes 665600 | tf_op jit(solution)/shard_map/dot_general | solution.py:80
  263.1 8.9 %fusion.80 = f32[160,512]{1,0:T(8,128)} fusion(bf16[160,1024]{1,0:T(8,128)(2,1)S(1)} %copy-done.5, s32[512]{0:T(512)S(1)} %iota_add_fusion.4, s32[1024]{0:T(1024)S(1)} %copy-done.6, f32[1024]{0:T(1024)S(1)} %get-tuple-element.20), kind=kOutput, calls=%fused_computation.179 | convolution fusion | flops 176160768 | bytes 665600 | tf_op jit(solution)/shard_map/dot_general | solution.py:77
  272.0 9.1 %fusion.89 = f32[160,512]{1,0:T(8,128)} fusion(bf16[160,1024]{1,0:T(8,128)(2,1)S(1)} %copy-done.5, f32[1024]{0:T(1024)S(1)} %get-tuple-element.18, s32[512]{0:T(512)S(1)} %iota_add_fusion.3, s32[1024]{0:T(1024)S(1)} %copy-done.6), kind=kOutput, calls=%fused_computation.188 | convolution fusion | flops 176160768 | bytes 665600 | tf_op jit(solution)/shard_map/dot_general | solution.py:80
  281.2 8.7 %fusion.81 = f32[160,512]{1,0:T(8,128)} fusion(bf16[160,1024]{1,0:T(8,128)(2,1)S(1)} %copy-done.5, s32[512]{0:T(512)S(1)} %iota_add_fusion.3, s32[1024]{0:T(1024)S(1)} %copy-done.6, f32[1024]{0:T(1024)S(1)} %get-tuple-element.20), kind=kOutput, calls=%fused_computation.180 | convolution fusion | flops 176160768 | bytes 665600 | tf_op jit(solution)/shard_map/dot_general | solution.py:77
  289.9 8.9 %fusion.90 = f32[160,512]{1,0:T(8,128)} fusion(bf16[160,1024]{1,0:T(8,128)(2,1)S(1)} %copy-done.5, f32[1024]{0:T(1024)S(1)} %get-tuple-element.18, s32[512]{0:T(512)S(1)} %iota_add_fusion.2, s32[1024]{0:T(1024)S(1)} %copy-done.6), kind=kOutput, calls=%fused_computation.189 | convolution fusion | flops 176160768 | bytes 665600 | tf_op jit(solution)/shard_map/dot_general | solution.py:80
  298.8 8.9 %fusion.82 = f32[160,512]{1,0:T(8,128)} fusion(bf16[160,1024]{1,0:T(8,128)(2,1)S(1)} %copy-done.5, s32[512]{0:T(512)S(1)} %iota_add_fusion.2, s32[1024]{0:T(1024)S(1)} %copy-done.6, f32[1024]{0:T(1024)S(1)} %get-tuple-element.20), kind=kOutput, calls=%fused_computation.181 | convolution fusion | flops 176160768 | bytes 665600 | tf_op jit(solution)/shard_map/dot_general | solution.py:77
  307.7 8.7 %fusion.91 = f32[160,512]{1,0:T(8,128)} fusion(bf16[160,1024]{1,0:T(8,128)(2,1)S(1)} %copy-done.5, f32[1024]{0:T(1024)S(1)} %get-tuple-element.18, s32[512]{0:T(512)S(1)} %iota_add_fusion.1, s32[1024]{0:T(1024)S(1)} %copy-done.6), kind=kOutput, calls=%fused_computation.190 | convolution fusion | flops 176160768 | bytes 665600 | tf_op jit(solution)/shard_map/dot_general | solution.py:80
  316.5 9.2 %fusion.83 = f32[160,512]{1,0:T(8,128)} fusion(bf16[160,1024]{1,0:T(8,128)(2,1)S(1)} %copy-done.5, s32[512]{0:T(512)S(1)} %iota_add_fusion.1, s32[1024]{0:T(1024)S(1)} %copy-done.6, f32[1024]{0:T(1024)S(1)} %get-tuple-element.20), kind=kOutput, calls=%fused_computation.182 | convolution fusion | flops 176160768 | bytes 665600 | tf_op jit(solution)/shard_map/dot_general | solution.py:77
  325.6 8.9 %fusion.92 = f32[160,512]{1,0:T(8,128)} fusion(bf16[160,1024]{1,0:T(8,128)(2,1)S(1)} %copy-done.5, f32[1024]{0:T(1024)S(1)} %get-tuple-element.18, s32[512]{0:T(512)S(1)} %iota_add_fusion, s32[1024]{0:T(1024)S(1)} %copy-done.6), kind=kOutput, calls=%fused_computation.191 | convolution fusion | flops 176160768 | bytes 665600 | tf_op jit(solution)/shard_map/dot_general | solution.py:80
  334.5 8.7 %fusion.84 = f32[160,512]{1,0:T(8,128)} fusion(bf16[160,1024]{1,0:T(8,128)(2,1)S(1)} %copy-done.5, s32[512]{0:T(512)S(1)} %iota_add_fusion, s32[1024]{0:T(1024)S(1)} %copy-done.6, f32[1024]{0:T(1024)S(1)} %get-tuple-element.20), kind=kOutput, calls=%fused_computation.183 | convolution fusion | flops 176160768 | bytes 665600 | tf_op jit(solution)/shard_map/dot_general | solution.py:77
  351.0 9.1 %fusion.62 = bf16[160,4096]{1,0:T(8,128)(2,1)S(1)} fusion(f32[160,512]{1,0:T(8,128)} %fusion.85, bf16[160,1024]{1,0:T(8,128)(2,1)} %reshape.139, f32[1024]{0:T(1024)S(1)} %get-tuple-element.18, s32[1024]{0:T(1024)S(1)} %copy-done.6), kind=kOutput, calls=%fused_computation.161 | convolution fusion | flops 176324608 | bytes 827392 | tf_op jit(solution)/shard_map/dot_general | solution.py:80
  384.5 8.4 %fusion.70 = bf16[160,4096]{1,0:T(8,128)(2,1)S(1)} fusion(bf16[160,4096]{1,0:T(8,128)(2,1)S(1)} %fusion.68, f32[160,512]{1,0:T(8,128)S(1)} %copy-done.18, bf16[160,1024]{1,0:T(8,128)(2,1)S(1)} %copy-done.3, f32[1024]{0:T(1024)S(1)} %get-tuple-element.18, s32[512]{0:T(512)S(1)} %iota_add_fusion.3, s32[1024]{0:T(1024)S(1)} %copy-done.6), kind=kOutput, calls=%fused_computation.169 | convolution fusion | flops 176324608 | bytes 829440 | tf_op jit(solution)/shard_map/dot_general | solution.py:80
  409.0 8.8 %fusion.76 = bf16[160,4096]{1,0:T(8,128)(2,1)S(1)} fusion(bf16[160,4096]{1,0:T(8,128)(2,1)S(1)} %fusion.74, f32[160,512]{1,0:T(8,128)S(1)} %copy-done.15, bf16[160,1024]{1,0:T(8,128)(2,1)S(1)} %copy-done.3, f32[1024]{0:T(1024)S(1)} %get-tuple-element.18, s32[512]{0:T(512)S(1)} %iota_add_fusion, s32[1024]{0:T(1024)S(1)} %copy-done.6), kind=kOutput, calls=%fused_computation.175 | convolution fusion | flops 176324608 | bytes 829440 | tf_op jit(solution)/shard_map/dot_general | solution.py:80
  428.2 8.2 %fusion.48 = bf16[160,4096]{1,0:T(8,128)(2,1)S(1)} fusion(bf16[160,4096]{1,0:T(8,128)(2,1)S(1)} %fusion.46, f32[160,512]{1,0:T(8,128)S(1)} %copy-done.14, bf16[160,1024]{1,0:T(8,128)(2,1)S(1)} %copy-done.4, f32[1024]{0:T(1024)S(1)} %get-tuple-element.19, s32[512]{0:T(512)S(1)} %iota_add_fusion.6, s32[1024]{0:T(1024)S(1)} %copy-done.6), kind=kOutput, calls=%fused_computation.147 | convolution fusion | flops 176324608 | bytes 829440 | tf_op jit(solution)/shard_map/dot_general | solution.py:77
  436.4 8.2 %fusion.50 = bf16[160,4096]{1,0:T(8,128)(2,1)S(1)} fusion(bf16[160,4096]{1,0:T(8,128)(2,1)S(1)} %fusion.48, f32[160,512]{1,0:T(8,128)S(1)} %copy-done.13, bf16[160,1024]{1,0:T(8,128)(2,1)S(1)} %copy-done.4, f32[1024]{0:T(1024)S(1)} %get-tuple-element.19, s32[512]{0:T(512)S(1)} %iota_add_fusion.5, s32[1024]{0:T(1024)S(1)} %copy-done.6), kind=kOutput, calls=%fused_computation.149 | convolution fusion | flops 176324608 | bytes 829440 | tf_op jit(solution)/shard_map/dot_general | solution.py:77
  452.7 8.4 %fusion.54 = bf16[160,4096]{1,0:T(8,128)(2,1)S(1)} fusion(bf16[160,4096]{1,0:T(8,128)(2,1)S(1)} %fusion.52, f32[160,512]{1,0:T(8,128)S(1)} %copy-done.11, bf16[160,1024]{1,0:T(8,128)(2,1)S(1)} %copy-done.4, f32[1024]{0:T(1024)S(1)} %get-tuple-element.19, s32[512]{0:T(512)S(1)} %iota_add_fusion.3, s32[1024]{0:T(1024)S(1)} %copy-done.6), kind=kOutput, calls=%fused_computation.153 | convolution fusion | flops 176324608 | bytes 829440 | tf_op jit(solution)/shard_map/dot_general | solution.py:77
  477.4 8.2 %fusion.60 = bf16[160,4096]{1,0:T(8,128)(2,1)S(1)} fusion(bf16[160,4096]{1,0:T(8,128)(2,1)S(1)} %fusion.58, f32[160,512]{1,0:T(8,128)S(1)} %copy-done.8, bf16[160,1024]{1,0:T(8,128)(2,1)S(1)} %copy-done.4, f32[1024]{0:T(1024)S(1)} %get-tuple-element.19, s32[512]{0:T(512)S(1)} %iota_add_fusion, s32[1024]{0:T(1024)S(1)} %copy-done.6), kind=kOutput, calls=%fused_computation.159 | convolution fusion | flops 176324608 | bytes 829440 | tf_op jit(solution)/shard_map/dot_general | solution.py:77
  (109 shorter events, 156.5 us)
Async XLA Ops:
  0.7 6.5 %copy-start.2 = (bf16[1,16,10,2,1024]{4,3,2,1,0:T(2,128)(2,1)S(1)}, bf16[1,16,10,2,1024]{4,3,2,1,0:T(2,128)(2,1)}, u32[]{:S(2)}) copy-start(bf16[1,16,10,2,1024]{4,3,2,1,0:T(2,128)(2,1)} %param.5) | copy-start | bytes 1966084
  0.7 7.2 %copy-start.7 = (s32[2,16]{1,0:T(2,128)S(1)}, s32[2,16]{1,0:T(2,128)}, u32[]{:S(2)}) copy-start(s32[2,16]{1,0:T(2,128)} %param.8) | copy-start | bytes 388
  63.5 18.2 %copy-start.6 = (s32[1024]{0:T(1024)S(1)}, s32[1024]{0:T(1024)}, u32[]{:S(2)}) copy-start(s32[1024]{0:T(1024)} %param.9) | copy-start | bytes 12292
  81.9 5.3 %copy-start = (bf16[16,64,16,1,64]{4,3,2,1,0:T(2,128)(2,1)S(1)}, bf16[16,64,16,1,64]{4,3,2,1,0:T(2,128)(2,1)}, u32[]{:S(2)}) copy-start(bf16[16,64,16,1,64]{4,3,2,1,0:T(2,128)(2,1)} %get-tuple-element.11) | copy-start | bytes 6291460
  81.9 10.2 %slice-start.2 = ((s8[8388608]{0:T(1024)(128)(4,1)}), s8[4194304]{0:T(1024)(128)(4,1)S(1)}, s32[]{:S(2)}) async-start(s8[8388608]{0:T(1024)(128)(4,1)} %bitcast.133), calls=%async_computation.4 | async-start | bytes 8388608
  86.6 5.5 %copy-start.1 = (bf16[16,10,2,16,64]{4,1,2,3,0:T(8,128)(2,1)}, bf16[16,10,2,16,64]{4,1,2,3,0:T(8,128)(2,1)S(1)}, u32[]{:S(2)}) copy-start(bf16[16,10,2,16,64]{4,1,2,3,0:T(8,128)(2,1)S(1)} %convert_bitcast_fusion) | copy-start | bytes 1966084
  86.6 5.5 %slice-start.3 = ((s8[8388608]{0:T(1024)(128)(4,1)}), s8[4194304]{0:T(1024)(128)(4,1)S(1)}, s32[]{:S(2)}) async-start(s8[8388608]{0:T(1024)(128)(4,1)} %bitcast.133), calls=%async_computation.5 | async-start | bytes 8388608
  87.3 14.2 %slice-start.4 = ((s8[8388608]{0:T(1024)(128)(4,1)}), s8[4194304]{0:T(1024)(128)(4,1)S(1)}, s32[]{:S(2)}) async-start(s8[8388608]{0:T(1024)(128)(4,1)} %bitcast.135), calls=%async_computation.6 | async-start | bytes 8388608
  92.1 9.4 %slice-start.5 = ((s8[8388608]{0:T(1024)(128)(4,1)}), s8[4194304]{0:T(1024)(128)(4,1)S(1)}, s32[]{:S(2)}) async-start(s8[8388608]{0:T(1024)(128)(4,1)} %bitcast.135), calls=%async_computation.7 | async-start | bytes 8388608
  92.1 12.4 %slice-start = ((s8[8388608]{0:T(1024)(128)(4,1)}), s8[4194304]{0:T(1024)(128)(4,1)S(1)}, s32[]{:S(2)}) async-start(s8[8388608]{0:T(1024)(128)(4,1)} %bitcast.131), calls=%async_computation.2 | async-start | bytes 8388608
  99.1 5.4 %slice-start.1 = ((s8[8388608]{0:T(1024)(128)(4,1)}), s8[4194304]{0:T(1024)(128)(4,1)S(1)}, s32[]{:S(2)}) async-start(s8[8388608]{0:T(1024)(128)(4,1)} %bitcast.131), calls=%async_computation.3 | async-start | bytes 8388608
  132.4 24.3 %all-to-all-start = ((bf16[64,2,2560]{2,1,0:T(2,128)(2,1)}), bf16[64,2,2560]{2,1,0:T(2,128)(2,1)S(1)}, u32[]{:S(2)}, u32[]{:S(2)}) async-start(bf16[64,2,2560]{2,1,0:T(2,128)(2,1)} %reshape.149), calls=%async_computation | async-start | bytes 1310720 | tf_op jit(solution)/shard_map/all_to_all | solution.py:47
  173.3 14.9 %all-to-all-start.1 = ((bf16[2,2,81920]{2,1,0:T(2,128)(2,1)}), bf16[2,2,81920]{2,1,0:T(2,128)(2,1)S(1)}, u32[]{:S(2)}, u32[]{:S(2)}) async-start(bf16[2,2,81920]{2,1,0:T(2,128)(2,1)} %reshape.151), calls=%async_computation.1 | async-start | bytes 1310720 | tf_op jit(solution)/shard_map/all_to_all | solution.py:48
  200.0 9.9 %copy-start.5 = (bf16[160,1024]{1,0:T(8,128)(2,1)S(1)}, bf16[160,1024]{1,0:T(8,128)(2,1)}, u32[]{:S(2)}) copy-start(bf16[160,1024]{1,0:T(8,128)(2,1)} %reshape.138) | copy-start | bytes 983044
  351.0 9.2 %copy-start.3 = (bf16[160,1024]{1,0:T(8,128)(2,1)S(1)}, bf16[160,1024]{1,0:T(8,128)(2,1)}, u32[]{:S(2)}) copy-start(bf16[160,1024]{1,0:T(8,128)(2,1)} %reshape.139) | copy-start | bytes 983044
  351.0 9.2 %copy-start.20 = (f32[160,512]{1,0:T(8,128)S(1)}, f32[160,512]{1,0:T(8,128)}, u32[]{:S(2)}) copy-start(f32[160,512]{1,0:T(8,128)} %fusion.86) | copy-start | bytes 983044
  360.1 8.1 %copy-start.21 = (f32[160,512]{1,0:T(8,128)S(1)}, f32[160,512]{1,0:T(8,128)}, u32[]{:S(2)}) copy-start(f32[160,512]{1,0:T(8,128)} %fusion.87) | copy-start | bytes 983044
  368.3 8.2 %copy-start.19 = (f32[160,512]{1,0:T(8,128)S(1)}, f32[160,512]{1,0:T(8,128)}, u32[]{:S(2)}) copy-start(f32[160,512]{1,0:T(8,128)} %fusion.88) | copy-start | bytes 983044
  376.5 8.0 %copy-start.18 = (f32[160,512]{1,0:T(8,128)S(1)}, f32[160,512]{1,0:T(8,128)}, u32[]{:S(2)}) copy-start(f32[160,512]{1,0:T(8,128)} %fusion.89) | copy-start | bytes 983044
  384.5 8.4 %copy-start.17 = (f32[160,512]{1,0:T(8,128)S(1)}, f32[160,512]{1,0:T(8,128)}, u32[]{:S(2)}) copy-start(f32[160,512]{1,0:T(8,128)} %fusion.90) | copy-start | bytes 983044
  392.9 8.1 %copy-start.16 = (f32[160,512]{1,0:T(8,128)S(1)}, f32[160,512]{1,0:T(8,128)}, u32[]{:S(2)}) copy-start(f32[160,512]{1,0:T(8,128)} %fusion.91) | copy-start | bytes 983044
  401.0 8.0 %copy-start.15 = (f32[160,512]{1,0:T(8,128)S(1)}, f32[160,512]{1,0:T(8,128)}, u32[]{:S(2)}) copy-start(f32[160,512]{1,0:T(8,128)} %fusion.92) | copy-start | bytes 983044
  418.3 1.8 copy-start.4
  418.3 1.8 copy-start.22
  420.1 8.1 %copy-start.14 = (f32[160,512]{1,0:T(8,128)S(1)}, f32[160,512]{1,0:T(8,128)}, u32[]{:S(2)}) copy-start(f32[160,512]{1,0:T(8,128)} %fusion.78) | copy-start | bytes 983044
  428.2 8.2 %copy-start.13 = (f32[160,512]{1,0:T(8,128)S(1)}, f32[160,512]{1,0:T(8,128)}, u32[]{:S(2)}) copy-start(f32[160,512]{1,0:T(8,128)} %fusion.79) | copy-start | bytes 983044
  436.4 8.3 %copy-start.12 = (f32[160,512]{1,0:T(8,128)S(1)}, f32[160,512]{1,0:T(8,128)}, u32[]{:S(2)}) copy-start(f32[160,512]{1,0:T(8,128)} %fusion.80) | copy-start | bytes 983044
  444.6 8.0 %copy-start.11 = (f32[160,512]{1,0:T(8,128)S(1)}, f32[160,512]{1,0:T(8,128)}, u32[]{:S(2)}) copy-start(f32[160,512]{1,0:T(8,128)} %fusion.81) | copy-start | bytes 983044
  452.7 8.4 %copy-start.10 = (f32[160,512]{1,0:T(8,128)S(1)}, f32[160,512]{1,0:T(8,128)}, u32[]{:S(2)}) copy-start(f32[160,512]{1,0:T(8,128)} %fusion.82) | copy-start | bytes 983044
  461.1 8.2 %copy-start.9 = (f32[160,512]{1,0:T(8,128)S(1)}, f32[160,512]{1,0:T(8,128)}, u32[]{:S(2)}) copy-start(f32[160,512]{1,0:T(8,128)} %fusion.83) | copy-start | bytes 983044
  469.3 8.0 %copy-start.8 = (f32[160,512]{1,0:T(8,128)S(1)}, f32[160,512]{1,0:T(8,128)}, u32[]{:S(2)}) copy-start(f32[160,512]{1,0:T(8,128)} %fusion.84) | copy-start | bytes 983044
where the time goes:
time: 496 us; the launch traced here: 488 us
  matrix products  302 us (61%)
  local copies, waits for them, and re-layouts  144 us (29%)
  waiting for transfers between devices  24.1 us (5%)
  starting transfers between devices  14.9 us (3%)
    dot_general x8, matrix products, body(): jnp.dot(real_left, sin_turned, preferred_element_type=jnp.float32)  72.4 us
    dot_general x8, matrix products, body(): jnp.dot(real_left, cos_value, preferred_element_type=jnp.float32)  70.8 us
    dot_general x8, matrix products, body(): jnp.dot(imag_left, cos_turned, preferred_element_type=jnp.float32)  66.6 us
    dot_general x8, matrix products, body(): jnp.dot(imag_left, sin_value, preferred_element_type=jnp.float32)  65.4 us
    slice x2, local copies, waits for them, and re-layouts, body(): factors[:, :, :, 0]  36 us
    another operation x2, local copies, waits for them, and re-layouts, body(): factors = level_factors[0, level].reshape(m_dev, rank, nblock, 2, rank)  31.7 us
    unnamed x65, local copies, waits for them, and re-layouts  27.2 us
    all_to_all x1, waiting for transfers between devices, body(): lax.all_to_all(partial_value, 'ma', split_axis=4, concat_axis=0, tiled=True)  13.8 us
  transfers between devices with their start and end apart: 2, of which 2 were waited for; matrix products, arithmetic and copies ran while one was open for 0% of the time, Pallas kernels for 0%

commit v1 on v0

v1 whole, which is shorter than its diff:
```python
import functools
import math

import jax
import jax.numpy as jnp
import numpy as np
from jax import lax
from jax.experimental import pallas as pl
from jax.experimental.pallas import tpu as pltpu
from jax.sharding import PartitionSpec as P

NLON = 4096
K = 64
NB = 16
NW = 16
NF = 10
M = 1024
LANES = 384
F32 = jnp.float32
BF16 = jnp.bfloat16
MESH = pl.DeviceIdType.MESH
NT = (((1,), (1,)), ((), ()))
TILE_WAVES = ((0, 6), (6, 12), (12, 16))


def target(g):
    return {"ma": g // 2, "ha": g % 2}


def xor_bits(a, b, bits):
    out = 0
    for i in range(bits):
        out = out + ((a // (1 << i) + b // (1 << i)) % 2) * (1 << i)
    return out


def iota(shape, dim):
    return lax.broadcasted_iota(jnp.int32, shape, dim)


def keep_waves(block, masks):
    return jnp.concatenate([jnp.where(m, block, jnp.zeros_like(block)) for m in masks], axis=0)


def synth_kernel(
    partners, waves, y_hbm, s_hbm, l_hbm, recv, yv, yf, zin, z0, z1, sv, lv, perm, send, in_sem, send_sem, recv_sem, own_sem
):
    ma = lax.axis_index("ma")
    ha = lax.axis_index("ha")
    me = ma * 2 + ha
    slot = ha * 64 + ma

    loads = [
        pltpu.make_async_copy(y_hbm, yv, in_sem.at[0]),
        pltpu.make_async_copy(s_hbm, sv, in_sem.at[1]),
        pltpu.make_async_copy(l_hbm.at[0], lv.at[0], in_sem.at[2]),
        pltpu.make_async_copy(l_hbm.at[1], lv.at[1], in_sem.at[3]),
    ]
    for load in loads:
        load.start()

    barrier = pltpu.get_barrier_semaphore()

    def greet(step, carry):
        g = (me + step) % 128
        pl.semaphore_signal(barrier, inc=1, device_id=target(g), device_id_type=MESH)
        return carry

    lax.fori_loop(1, 128, greet, 0)

    col = iota((1, LANES), 1)
    wave = col % 16
    fr = col // 16
    tile = (wave >= 6).astype(jnp.int32) + (wave >= 12).astype(jnp.int32)
    source = tile * 128 + (fr % 2) * 64 + (wave - 6 * tile) * 10 + fr // 2
    source = jnp.where(col < 320, source, -1)
    perm[...] = (iota((LANES, LANES), 0) == source).astype(F32).astype(BF16)
    eye = (iota((128, 128), 0) == iota((128, 128), 1)).astype(F32).astype(BF16)
    lane_wave = (iota((128, 128), 1) % 64) // 10
    masks = [lane_wave == w for w in range(6)]

    yf[pl.ds(2560, 512), :] = jnp.zeros((512, 128), F32)
    loads[0].wait()
    degree = 2 * ((iota((16, 128), 0) // 2) * 128 + iota((16, 128), 1)) + ha
    for w in range(NW):
        keep = degree <= (M - 1) - waves[ma * NW + w]
        for f in range(NF):
            row = (w * NF + f) * 16
            yf[pl.ds(row, 16), :] = jnp.where(keep, yv[pl.ds(row, 16), :].astype(F32), 0.0)
    for j in range(8):
        for t in range(3):
            rows = [yf[pl.ds(t * 960 + 2 * j + part, 64, stride=16), :] for part in range(2)]
            block = jnp.concatenate(rows, axis=0).astype(BF16)
            turned = lax.dot_general(eye, block, NT, preferred_element_type=F32)
            zin[j, :, pl.ds(t * 128, 128)] = turned.astype(BF16)

    loads[1].wait()
    low = iota((64, 128), 1) < 64

    def section(j, carry):
        lanes = pl.ds(pl.multiple_of(j * 128, 128), 128)
        for t, (first, last) in enumerate(TILE_WAVES):
            left = []
            for w in range(first, last):
                factor = sv[w, :, lanes]
                zero = jnp.zeros_like(factor)
                left.append(jnp.concatenate([jnp.where(low, factor, zero), jnp.where(low, zero, factor)], axis=0))
            right = keep_waves(zin[j, :, pl.ds(t * 128, 128)], masks[: last - first])
            out = jnp.dot(jnp.concatenate(left, axis=1), right, preferred_element_type=F32).astype(BF16)
            z0[2 * j, :, pl.ds(t * 128, 128)] = out[:64]
            z0[2 * j + 1, :, pl.ds(t * 128, 128)] = out[64:]
        return carry

    lax.fori_loop(0, 8, section, 0)

    def level(l, b, z):
        other = partners[l, b]
        lanes = pl.ds(pl.multiple_of(b * 128, 128), 128)
        outs = []
        for t, (first, last) in enumerate(TILE_WAVES):
            left = jnp.concatenate([lv[l, w, :, lanes] for w in range(first, last)], axis=1)
            both = jnp.concatenate([z[b, :, pl.ds(t * 128, 128)], z[other, :, pl.ds(t * 128, 128)]], axis=0)
            right = keep_waves(both, masks[: last - first])
            outs.append(jnp.dot(left, right, preferred_element_type=F32).astype(BF16))
        return outs

    loads[2].wait()

    def first_level(b, carry):
        for t, out in enumerate(level(0, b, z0)):
            z1[b, :, pl.ds(t * 128, 128)] = out
        return carry

    lax.fori_loop(0, NB, first_level, 0)
    loads[3].wait()
    pl.semaphore_wait(barrier, 127)

    own = pltpu.make_async_copy(send.at[me], recv.at[slot], own_sem)
    low_bits = [me % 2, (me // 2) % 2, (me // 4) % 2]

    def last_level(step, carry):
        b = xor_bits(me // 8, step, 4)
        state = jnp.concatenate(level(1, b, z1), axis=1)
        moved = jnp.dot(state, perm[...], preferred_element_type=F32)
        for t in range(3):
            send[pl.ds(b * 8, 8), t] = moved[:, t * 128 : (t + 1) * 128].reshape(8, 8, 128).astype(BF16)
        for r in range(8):
            g = b * 8
            for i in range(3):
                g = g + (1 - low_bits[i] if (r >> i) & 1 else low_bits[i]) * (1 << i)

            def go():
                pltpu.make_async_remote_copy(
                    send.at[g], recv.at[slot], send_sem, recv_sem, device_id=target(g), device_id_type=MESH
                ).start()

            if r == 0:
                pl.when(step > 0)(go)
                pl.when(step == 0)(own.start)
            else:
                go()
        return carry

    lax.fori_loop(0, NB, last_level, 0)
    own.wait()
    pltpu.make_async_remote_copy(
        send.at[pl.ds(0, 127)], recv.at[pl.ds(0, 127)], send_sem, recv_sem, device_id=target(me), device_id_type=MESH
    ).wait()


def synth(partners, waves, y, s, l):
    smem = pl.BlockSpec(memory_space=pltpu.SMEM)
    hbm = pl.BlockSpec(memory_space=pl.ANY)
    return pl.pallas_call(
        synth_kernel,
        out_shape=jax.ShapeDtypeStruct((128, 3, 8, 128), BF16),
        in_specs=[smem, smem, hbm, hbm, hbm],
        out_specs=hbm,
        scratch_shapes=[
            pltpu.VMEM((2560, 128), BF16),
            pltpu.VMEM((3072, 128), F32),
            pltpu.VMEM((8, 128, LANES), BF16),
            pltpu.VMEM((NB, K, LANES), BF16),
            pltpu.VMEM((NB, K, LANES), BF16),
            pltpu.VMEM((NW, K, 1024), BF16),
            pltpu.VMEM((2, NW, K, 2048), BF16),
            pltpu.VMEM((LANES, LANES), BF16),
            pltpu.VMEM((128, 3, 8, 128), BF16),
            pltpu.SemaphoreType.DMA((4,)),
            pltpu.SemaphoreType.DMA,
            pltpu.SemaphoreType.DMA,
            pltpu.SemaphoreType.DMA,
        ],
        compiler_params=pltpu.CompilerParams(collective_id=0, has_side_effects=True, vmem_limit_bytes=40 << 20),
    )(partners, waves, y, s, l)


def dft_tables():
    a = np.arange(128)
    out = np.zeros((4, 8, 256, 256), np.float64)
    for c in range(4):
        lon = 128 * c + np.arange(128)
        for b in range(8):
            angle = 2.0 * math.pi * (((8 * a + b)[:, None] * lon[None, :]) % NLON) / NLON
            cos, sin = np.cos(angle), np.sin(angle)
            out[c, b] = np.block([[cos, sin], [-sin, cos]])
    return out.astype(np.float32)


def grid_kernel(recv, waves, table_hbm, grid_hbm, slope_hbm, wf, left, table, g, out, in_sem, out_sem):
    load = pltpu.make_async_copy(table_hbm, table, in_sem)
    load.start()
    group = iota((8, 128), 1) // 16

    def spread(j, carry):
        lanes = pl.ds(pl.multiple_of(j * 128, 128), 128)
        for q in range(3):
            sides = []
            for p in range(2):
                rows = [recv[p * 64 + 8 * j + i, q].astype(F32) for i in range(8)]
                for d in (4, 2, 1):
                    upper = (group // d) % 2 == 1
                    new = list(rows)
                    for i in range(len(rows)):
                        if i & d or i + d >= len(rows):
                            continue
                        one, two = rows[i], rows[i + d]
                        new[i] = jnp.where(upper, pltpu.roll(two, 16 * d, 1), one)
                        new[i + d] = jnp.where(upper, two, pltpu.roll(one, 128 - 16 * d, 1))
                    rows = new
                    if q == 2 and d == 4:
                        rows = rows[:4]
                sides.append(rows)
            for i in range(len(sides[0])):
                fr = q * 8 + i
                even, odd = sides[0][i], sides[1][i]
                row = (fr % 2) * 160 + (fr // 2) * 8
                wf[pl.ds(row, 8), lanes] = even + odd
                wf[pl.ds(row + 80, 8), lanes] = even - odd
        return carry

    lax.fori_loop(0, 8, spread, 0)

    spectra = wf[...].astype(BF16)
    slot_wave = waves[...]
    for b in range(8):
        k = 8 * iota((128, 1), 0) + b
        weight = jnp.where(k > 0, 2.0, 1.0)
        pick = jnp.where(slot_wave == k, weight, 0.0).astype(BF16)
        moved = lax.dot_general(spectra, pick, NT, preferred_element_type=F32)
        real, imag = moved[:160], moved[160:]
        scale = (8 * iota((1, 128), 1) + b).astype(F32) * (1.0 / M)
        left[b, pl.ds(0, 160), pl.ds(0, 128)] = real.astype(BF16)
        left[b, pl.ds(0, 160), pl.ds(128, 128)] = imag.astype(BF16)
        left[b, pl.ds(160, 160), pl.ds(0, 128)] = (-scale * imag).astype(BF16)
        left[b, pl.ds(160, 160), pl.ds(128, 128)] = (scale * real).astype(BF16)

    load.wait()
    root = math.sqrt(0.5)
    copies = []
    for c in range(4):
        for b in range(8):
            g[b] = jnp.dot(left[b], table[c, b], preferred_element_type=F32)

        def combine(i, carry, c=c):
            rows = pl.ds(pl.multiple_of(i * 16, 16), 16)
            re = [g[b, rows, pl.ds(0, 128)] for b in range(8)]
            im = [None if b in (0, 4) else g[b, rows, pl.ds(128, 128)] for b in range(8)]
            plus, minus = re[0] + re[4], re[0] - re[4]
            r26, i26 = re[2] + re[6], im[6] - im[2]
            even = [plus + r26, minus + i26, plus - r26, minus - i26]
            r17, r35 = re[1] + re[7], re[3] + re[5]
            i71, i53 = im[7] - im[1], im[5] - im[3]
            rr, ii = root * (r17 - r35), root * (i71 + i53)
            odd = [r17 + r35, ii + rr, i71 - i53, ii - rr]
            for j in range(4):
                out[rows, pl.ds(512 * j + 128 * c, 128)] = (even[j] + odd[j]).astype(BF16)
                out[rows, pl.ds(512 * j + 2048 + 128 * c, 128)] = (even[j] - odd[j]).astype(BF16)
            return carry

        lax.fori_loop(0, 20, combine, 0)
        for j in range(8):
            lanes = pl.ds(512 * j + 128 * c, 128)
            for n, target_hbm in enumerate((grid_hbm, slope_hbm)):
                copy = pltpu.make_async_copy(out.at[pl.ds(160 * n, 160), lanes], target_hbm.at[:, lanes], out_sem.at[len(copies)])
                copy.start()
                copies.append(copy)
    for copy in copies:
        copy.wait()


def to_grid(recv, waves, table):
    vmem = pl.BlockSpec(memory_space=pltpu.VMEM)
    hbm = pl.BlockSpec(memory_space=pl.ANY)
    shape = jax.ShapeDtypeStruct((160, NLON), BF16)
    return pl.pallas_call(
        grid_kernel,
        out_shape=(shape, shape),
        in_specs=[vmem, vmem, hbm],
        out_specs=(hbm, hbm),
        scratch_shapes=[
            pltpu.VMEM((320, 1024), F32),
            pltpu.VMEM((8, 320, 256), BF16),
            pltpu.VMEM((4, 8, 256, 256), BF16),
            pltpu.VMEM((8, 320, 256), F32),
            pltpu.VMEM((320, NLON), BF16),
            pltpu.SemaphoreType.DMA,
            pltpu.SemaphoreType.DMA((64,)),
        ],
        compiler_params=pltpu.CompilerParams(vmem_limit_bytes=40 << 20),
    )(recv, waves, table)


def body(coefficients, section_factors, level_factors, partners, wave_ids):
    y = coefficients.reshape(NW * NF, 2, 2, 4, 128).transpose(0, 2, 3, 1, 4).reshape(NW * NF * 16, 128)
    recv = synth(partners, wave_ids, y, section_factors[0], level_factors[0])
    grid, slope = to_grid(recv, wave_ids.reshape(1, M), jnp.asarray(dft_tables(), BF16))
    shape = (2, NF, 8, NLON)
    return (
        grid.reshape(shape).transpose(0, 2, 1, 3),
        slope.reshape(shape).transpose(0, 2, 1, 3),
    )


def solution(mesh):
    in_specs = (
        P("ha", "ma", None, None, None),
        P("ha", "ma", None, None),
        P("ha", None, "ma", None, None),
        P(),
        P(),
    )
    out_specs = (P(None, ("ma", "ha"), None, None), P(None, ("ma", "ha"), None, None))
    return jax.shard_map(body, mesh=mesh, in_specs=in_specs, out_specs=out_specs, check_vma=False)
```

time: 496 us -> 53.5 us (0.11); the launches traced: 488 us -> 53.3 us
  matrix products: 302 us -> 0 us
  local copies, waits for them, and re-layouts: 144 us -> 7.42 us
  Pallas kernels: 0 us -> 45.2 us
  waiting for transfers between devices: 24.1 us -> 0 us
  starting transfers between devices: 14.9 us -> 0 us
    dot_general x39 -> x0, matrix products: 302 us -> none  [the longest x8 72.4 us: body(): jnp.dot(real_left, sin_turned, preferred_element_type=jnp.float32)]
    pallas_call x0 -> x2, Pallas kernels: none -> 45.2 us  [the longest x1 36.6 us: synth(): pl.pallas_call(synth_kernel, out_shape=jax.ShapeDtypeStruct((128, 3, 8, 1...]
    slice x3 -> x0, local copies, waits for them, and re-layouts: 42.1 us -> none  [the longest x2 36 us: body(): factors[:, :, :, 0]]
    another operation x3 -> x0, local copies, waits for them, and re-layouts: 38.2 us -> none  [the longest x2 31.7 us: body(): factors = level_factors[0, level].reshape(m_dev, rank, nblock, 2, rank)]
    all_to_all x2 -> x0, waiting for transfers between devices: 24.1 us -> none  [the longest x1 13.8 us: body(): lax.all_to_all(partial_value, 'ma', split_axis=4, concat_axis=0, tiled=True)]
    reshape x5 -> x0, local copies, waits for them, and re-layouts: 20.2 us -> none  [the longest x1 7.91 us: body(): partial_value = state.reshape(1, m_dev, nfield, 2, lath)]
    unnamed x65 -> x12, local copies, waits for them, and re-layouts: 27.2 us -> 7.42 us
    all_to_all x2 -> x0, starting transfers between devices: 14.9 us -> none  [the longest x1 10.3 us: body(): lax.all_to_all(partial_value, 'ma', split_axis=4, concat_axis=0, tiled=True)]
  transfers between devices with their start and end apart: 2 -> 0, of which waited for: 2 -> 0; matrix products, arithmetic and copies ran while one was open for 0% -> 0% of each run, Pallas kernels for 0% -> 0%
where the time goes in v1:
time: 53.5 us; the launch traced here: 53.3 us
  Pallas kernels  45.2 us (84%)
  local copies, waits for them, and re-layouts  7.42 us (14%)
  between operations  0.66 us (1%)
    pallas_call x1, Pallas kernels, synth(): pl.pallas_call(synth_kernel, out_shape=jax.ShapeDtypeStruct((128, 3, 8, 1...  36.6 us
    pallas_call x1, Pallas kernels, to_grid(): pl.pallas_call(grid_kernel, out_shape=(shape, shape), in_specs=[vmem, vme...  8.58 us
    unnamed x12, local copies, waits for them, and re-layouts  7.42 us

profile of v1, /device:TPU:1, one launch (start us, length us, event | category | flops | bytes accessed | tf_op | source)
XLA Modules:
  0.0 53.3 jit_solution(2836858600706749269)
XLA Ops:
  0.6 0.0 copy-start
  0.6 3.4 %copy-done = bf16[1,2,16,64,2048]{4,3,2,1,0:T(8,128)(2,1)S(1)} copy-done((bf16[1,2,16,64,2048]{4,3,2,1,0:T(8,128)(2,1)S(1)}, bf16[1,2,16,64,2048]{4,3,2,1,0:T(8,128)(2,1)}, u32[]{:S(2)}) %copy-start) | copy-done | bytes 8388632
  4.0 0.0 copy-start.2
  4.0 1.6 %copy-done.2 = bf16[1,16,64,1024]{3,2,1,0:T(8,128)(2,1)S(1)} copy-done((bf16[1,16,64,1024]{3,2,1,0:T(8,128)(2,1)S(1)}, bf16[1,16,64,1024]{3,2,1,0:T(8,128)(2,1)}, u32[]{:S(2)}) %copy-start.2) | copy-done | bytes 2097176
  5.6 0.0 copy-start.3
  5.6 1.1 %copy-done.3 = bf16[1,16,10,2,1024]{4,3,2,1,0:T(2,128)(2,1)S(1)} copy-done((bf16[1,16,10,2,1024]{4,3,2,1,0:T(2,128)(2,1)S(1)}, bf16[1,16,10,2,1024]{4,3,2,1,0:T(2,128)(2,1)}, u32[]{:S(2)}) %copy-start.3) | copy-done | bytes 655384
  6.7 0.0 copy-start.4
  6.7 0.7 %copy-done.4 = s32[1024]{0:T(1024)S(1)} copy-done((s32[1024]{0:T(1024)S(1)}, s32[1024]{0:T(1024)}, u32[]{:S(2)}) %copy-start.4) | copy-done | bytes 4120
  7.4 0.0 copy-start.5
  7.4 0.7 %copy-done.5 = s32[2,16]{1,0:T(2,128)S(1)} copy-done((s32[2,16]{1,0:T(2,128)S(1)}, s32[2,16]{1,0:T(2,128)}, u32[]{:S(2)}) %copy-start.5) | copy-done | bytes 152
  8.1 0.0 copy-start.1
  8.1 36.6 %shard_map.77.recv = bf16[128,3,8,128]{3,2,1,0:T(8,128)(2,1)S(1)} custom-call(s32[2,16]{1,0:T(2,128)S(1)} %copy-done.5, s32[1024]{0:T(1024)S(1)} %copy-done.4, bf16[2560,128]{1,0:T(8,128)(2,1)S(1)} %bitcast.16, bf16[16,64,1024]{2,1,0:T(8,128)(2,1)S(1)} %bitcast.15, bf16[2,16,64,2048]{3,2,1,0:T(8,128)(2,1)S(1)} %bitcast.14), custom_call_target="tpu_custom_call" | custom-call | tf_op jit(solution)/shard_map/pallas_call | solution.py:174
  44.7 0.0 copy-done.1
  44.7 8.6 %shard_map.78 = (bf16[160,4096]{1,0:T(8,128)(2,1)}, bf16[160,4096]{1,0:T(8,128)(2,1)}) custom-call(bf16[128,3,8,128]{3,2,1,0:T(8,128)(2,1)S(1)} %shard_map.77.recv, s32[1,1024]{1,0:T(1,128)S(1)} %bitcast.17, bf16[4,8,256,256]{3,2,1,0:T(8,128)(2,1)S(1)} %copy-done.1), custom_call_target="tpu_custom_call" | custom-call | tf_op jit(solution)/shard_map/pallas_call | solution.py:296
Async XLA Ops:
  0.6 3.4 %copy-start = (bf16[1,2,16,64,2048]{4,3,2,1,0:T(8,128)(2,1)S(1)}, bf16[1,2,16,64,2048]{4,3,2,1,0:T(8,128)(2,1)}, u32[]{:S(2)}) copy-start(bf16[1,2,16,64,2048]{4,3,2,1,0:T(8,128)(2,1)} %param.8) | copy-start | bytes 25165828
  4.0 1.6 %copy-start.2 = (bf16[1,16,64,1024]{3,2,1,0:T(8,128)(2,1)S(1)}, bf16[1,16,64,1024]{3,2,1,0:T(8,128)(2,1)}, u32[]{:S(2)}) copy-start(bf16[1,16,64,1024]{3,2,1,0:T(8,128)(2,1)} %param.7) | copy-start | bytes 6291460
  5.6 1.1 %copy-start.3 = (bf16[1,16,10,2,1024]{4,3,2,1,0:T(2,128)(2,1)S(1)}, bf16[1,16,10,2,1024]{4,3,2,1,0:T(2,128)(2,1)}, u32[]{:S(2)}) copy-start(bf16[1,16,10,2,1024]{4,3,2,1,0:T(2,128)(2,1)} %param.6) | copy-start | bytes 1966084
  6.7 0.7 %copy-start.4 = (s32[1024]{0:T(1024)S(1)}, s32[1024]{0:T(1024)}, u32[]{:S(2)}) copy-start(s32[1024]{0:T(1024)} %waves.1) | copy-start | bytes 12292
  7.4 0.7 %copy-start.5 = (s32[2,16]{1,0:T(2,128)S(1)}, s32[2,16]{1,0:T(2,128)}, u32[]{:S(2)}) copy-start(s32[2,16]{1,0:T(2,128)} %partners.1) | copy-start | bytes 388
  8.1 36.6 %copy-start.1 = (bf16[4,8,256,256]{3,2,1,0:T(8,128)(2,1)S(1)}, bf16[4,8,256,256]{3,2,1,0:T(8,128)(2,1)}, u32[]{:S(2)}) copy-start(bf16[4,8,256,256]{3,2,1,0:T(8,128)(2,1)} %constant.2.clone.table_hbm) | copy-start | bytes 12582916

commit v2 on v1

v2 whole, which is shorter than its diff:
```python
import functools
import math

import jax
import jax.numpy as jnp
import numpy as np
from jax import lax
from jax.experimental import pallas as pl
from jax.experimental.pallas import tpu as pltpu
from jax.sharding import PartitionSpec as P

NLON = 4096
K = 64
NB = 16
NW = 16
NF = 10
M = 1024
LANES = 384
F32 = jnp.float32
BF16 = jnp.bfloat16
MESH = pl.DeviceIdType.MESH
NT = (((1,), (1,)), ((), ()))
TILE_WAVES = ((0, 6), (6, 12), (12, 16))


def target(g):
    return {"ma": g // 2, "ha": g % 2}


def iota(shape, dim):
    return lax.broadcasted_iota(jnp.int32, shape, dim)


def keep_waves(block, masks):
    return jnp.concatenate([jnp.where(m, block, jnp.zeros_like(block)) for m in masks], axis=0)


ORDER = (5, 3, 7, 4, 1, 2, 6, 0)


def pick(bit, base):
    return 1 - base if bit else base


def synth_kernel(
    partners_hbm, waves_hbm, table_hbm, y_hbm, s_hbm, l_hbm, left,
    partners, waves, wave_rows, yv, yf, zin, z0, z1, sv, lv, perm, send, recv, acc, in_sem, send_sem, recv_sem, own_sem,
):
    ma = lax.axis_index("ma")
    ha = lax.axis_index("ha")
    me = ma * 2 + ha
    slot = ha * 64 + ma

    loads = [
        pltpu.make_async_copy(y_hbm, yv, in_sem.at[0]),
        pltpu.make_async_copy(waves_hbm, waves, in_sem.at[1]),
        pltpu.make_async_copy(partners_hbm, partners, in_sem.at[2]),
        pltpu.make_async_copy(table_hbm, wave_rows, in_sem.at[3]),
        pltpu.make_async_copy(s_hbm, sv, in_sem.at[4]),
        pltpu.make_async_copy(l_hbm.at[0], lv.at[0], in_sem.at[5]),
        pltpu.make_async_copy(l_hbm.at[1], lv.at[1], in_sem.at[6]),
    ]
    for load in loads[:6]:
        load.start()

    barrier = pltpu.get_barrier_semaphore()

    def greet(first, last):
        for step in range(max(first, 1), last):
            pl.semaphore_signal(barrier, inc=1, device_id=target((me + step) % 128), device_id_type=MESH)

    col = iota((1, LANES), 1)
    col = jnp.where(col < 320, col, col - 64)
    wave = col % 16
    fr = col // 16
    tile = (wave >= 6).astype(jnp.int32) + (wave >= 12).astype(jnp.int32)
    source = tile * 128 + (fr % 2) * 64 + (wave - 6 * tile) * 10 + fr // 2
    perm[...] = (iota((LANES, LANES), 0) == source).astype(F32).astype(BF16)
    eye = (iota((128, 128), 0) == iota((128, 128), 1)).astype(F32).astype(BF16)
    lane_wave = (iota((128, 128), 1) % 64) // 10
    masks = [lane_wave == w for w in range(6)]

    yf[pl.ds(2560, 512), :] = jnp.zeros((512, 128), F32)
    degree = 2 * ((iota((16, 128), 0) // 2) * 128 + iota((16, 128), 1)) + ha
    greet(0, 16)
    loads[1].wait()
    loads[0].wait()
    for w in range(NW):
        keep = degree <= (M - 1) - waves[ma * NW + w]
        for f in range(NF):
            row = (w * NF + f) * 16
            yf[pl.ds(row, 16), :] = jnp.where(keep, yv[pl.ds(row, 16), :].astype(F32), 0.0)
        greet(16 + 7 * w, 23 + 7 * w)
    for j in range(8):
        for t in range(3):
            rows = [yf[pl.ds(t * 960 + 2 * j + part, 64, stride=16), :] for part in range(2)]
            block = jnp.concatenate(rows, axis=0).astype(BF16)
            turned = lax.dot_general(eye, block, NT, preferred_element_type=F32)
            zin[j, :, pl.ds(t * 128, 128)] = turned.astype(BF16)

    loads[4].wait()
    loads[6].start()
    low = iota((64, 128), 1) < 64

    def section(j, carry):
        lanes = pl.ds(pl.multiple_of(j * 128, 128), 128)
        for t, (first, last) in enumerate(TILE_WAVES):
            halves = []
            for w in range(first, last):
                factor = sv[w, :, lanes]
                zero = jnp.zeros_like(factor)
                halves.append(jnp.concatenate([jnp.where(low, factor, zero), jnp.where(low, zero, factor)], axis=0))
            right = keep_waves(zin[j, :, pl.ds(t * 128, 128)], masks[: last - first])
            out = jnp.dot(jnp.concatenate(halves, axis=1), right, preferred_element_type=F32).astype(BF16)
            z0[2 * j, :, pl.ds(t * 128, 128)] = out[:64]
            z0[2 * j + 1, :, pl.ds(t * 128, 128)] = out[64:]
        return carry

    lax.fori_loop(0, 8, section, 0, unroll=2)

    def level(l, b, z):
        other = partners[l, b]
        lanes = pl.ds(pl.multiple_of(b * 128, 128), 128)
        outs = []
        for t, (first, last) in enumerate(TILE_WAVES):
            factors = jnp.concatenate([lv[l, w, :, lanes] for w in range(first, last)], axis=1)
            both = jnp.concatenate([z[b, :, pl.ds(t * 128, 128)], z[other, :, pl.ds(t * 128, 128)]], axis=0)
            right = keep_waves(both, masks[: last - first])
            outs.append(jnp.dot(factors, right, preferred_element_type=F32).astype(BF16))
        return outs

    loads[2].wait()
    loads[3].wait()
    loads[5].wait()

    def first_level(b, carry):
        for t, out in enumerate(level(0, b, z0)):
            z1[b, :, pl.ds(t * 128, 128)] = out
        return carry

    lax.fori_loop(0, NB, first_level, 0, unroll=4)
    loads[6].wait()
    pl.semaphore_wait(barrier, 127)

    own = pltpu.make_async_copy(send.at[me], recv.at[slot], own_sem)
    pair = me // 16
    low_bits = [me % 2, (me // 2) % 2, (me // 4) % 2, (me // 8) % 2]
    high = [pair % 2, (pair // 2) % 2, pair // 4]
    half = iota((16, 4, 128), 2) < 64

    def partner_pair(mask):
        return sum(pick((mask >> i) & 1, high[i]) * (1 << i) for i in range(3))

    for i, mask in enumerate(ORDER):
        p = partner_pair(mask)
        blocks = [level(1, 2 * p + k, z1) for k in range(2)]
        state = jnp.concatenate([jnp.concatenate(outs, axis=1) for outs in blocks], axis=0)
        moved = jnp.dot(state, perm[...], preferred_element_type=F32)
        groups = pl.ds(p * 16, 16)
        for t in range(3):
            rows = moved[:, t * 128 : (t + 1) * 128].reshape(16, 8, 128)
            if t < 2:
                send[groups, 2 * t] = rows[:, :4].astype(BF16)
                send[groups, 2 * t + 1] = rows[:, 4:].astype(BF16)
            else:
                send[groups, 4] = jnp.where(half, rows[:, :4], rows[:, 4:]).astype(BF16)
        for r in range(15, -1, -1):
            g = p * 16 + sum(pick((r >> n) & 1, low_bits[n]) * (1 << n) for n in range(4))
            if mask == 0 and r == 0:
                own.start()
            else:
                pltpu.make_async_remote_copy(
                    send.at[g], recv.at[slot], send_sem, recv_sem.at[i], device_id=target(g), device_id_type=MESH
                ).start()

    group = iota((8, 128), 1) // 16
    for i, mask in enumerate(ORDER):
        j = partner_pair(mask)
        slot_wave = wave_rows[pl.ds(j, 1), :]
        row = iota((M, 1), 0)
        k = 8 * (row % 128) + row // 128
        weight = jnp.where(k > 0, 2.0, 1.0)
        onehot = jnp.where(slot_wave == k, weight, 0.0).astype(BF16)
        count = 16 if mask else 15
        pltpu.make_async_remote_copy(
            send.at[pl.ds(0, count)], recv.at[pl.ds(0, count)], send_sem, recv_sem.at[i],
            device_id=target(me), device_id_type=MESH,
        ).wait_recv()
        if mask == 0:
            own.wait()
        parts = [[None] * 20, [None] * 20]
        for q in range(3):
            sides = []
            for p in range(2):
                rows = []
                for n in range(8):
                    message = recv.at[p * 64 + 8 * j + n]
                    if q < 2:
                        rows.append(jnp.concatenate([message[2 * q].astype(F32), message[2 * q + 1].astype(F32)], axis=0))
                    else:
                        packed = message[4].astype(F32)
                        both = jnp.concatenate([packed, packed], axis=0)
                        rows.append(jnp.where(iota((8, 128), 0) < 4, both, pltpu.roll(both, 64, 1)))
                for d in (4, 2, 1):
                    upper = (group // d) % 2 == 1
                    new = list(rows)
                    for n in range(len(rows)):
                        if n & d or n + d >= len(rows):
                            continue
                        one, two = rows[n], rows[n + d]
                        new[n] = jnp.where(upper, pltpu.roll(two, 16 * d, 1), one)
                        new[n + d] = jnp.where(upper, two, pltpu.roll(one, 128 - 16 * d, 1))
                    rows = new
                    if q == 2 and d == 4:
                        rows = rows[:4]
                sides.append(rows)
            for n, (even, odd) in enumerate(zip(*sides)):
                fr = q * 8 + n
                parts[fr % 2][fr // 2] = even + odd
                parts[fr % 2][10 + fr // 2] = even - odd
        spectra = jnp.concatenate(parts[0] + parts[1], axis=0).astype(BF16)
        for b in range(8):
            lanes = pl.ds(b * 128, 128)
            moved = lax.dot_general(spectra, onehot[b * 128 : (b + 1) * 128], NT, preferred_element_type=F32)
            if i > 0:
                moved = moved + acc[:, lanes]
            if i < 7:
                acc[:, lanes] = moved
            else:
                real, imag = moved[:160], moved[160:]
                scale = (8 * iota((1, 128), 1) + b).astype(F32) * (1.0 / M)
                left[b, pl.ds(0, 160), pl.ds(0, 128)] = real.astype(BF16)
                left[b, pl.ds(0, 160), pl.ds(128, 128)] = imag.astype(BF16)
                left[b, pl.ds(160, 160), pl.ds(0, 128)] = (-scale * imag).astype(BF16)
                left[b, pl.ds(160, 160), pl.ds(128, 128)] = (scale * real).astype(BF16)

    pltpu.make_async_remote_copy(
        send.at[pl.ds(0, 127)], recv.at[pl.ds(0, 127)], send_sem, recv_sem.at[0], device_id=target(me), device_id_type=MESH
    ).wait_send()


def synth(partners, waves, y, s, l):
    hbm = pl.BlockSpec(memory_space=pltpu.HBM)
    return pl.pallas_call(
        synth_kernel,
        out_shape=jax.ShapeDtypeStruct((8, 320, 256), BF16),
        in_specs=[hbm] * 6,
        out_specs=pl.BlockSpec(memory_space=pltpu.VMEM),
        scratch_shapes=[
            pltpu.SMEM((2, NB), jnp.int32),
            pltpu.SMEM((M,), jnp.int32),
            pltpu.VMEM((8, 128), jnp.int32),
            pltpu.VMEM((2560, 128), BF16),
            pltpu.VMEM((3072, 128), F32),
            pltpu.VMEM((8, 128, LANES), BF16),
            pltpu.VMEM((NB, K, LANES), BF16),
            pltpu.VMEM((NB, K, LANES), BF16),
            pltpu.VMEM((NW, K, 1024), BF16),
            pltpu.VMEM((2, NW, K, 2048), BF16),
            pltpu.VMEM((LANES, LANES), BF16),
            pltpu.VMEM((128, 5, 4, 128), BF16),
            pltpu.VMEM((128, 5, 4, 128), BF16),
            pltpu.VMEM((320, M), F32),
            pltpu.SemaphoreType.DMA((7,)),
            pltpu.SemaphoreType.DMA,
            pltpu.SemaphoreType.DMA((8,)),
            pltpu.SemaphoreType.DMA,
        ],
        compiler_params=pltpu.CompilerParams(collective_id=0, has_side_effects=True, vmem_limit_bytes=32 << 20),
    )(*[pltpu.with_memory_space_constraint(v, pltpu.HBM) for v in (partners, waves, waves.reshape(8, 128), y, s, l)])


def dft_tables():
    a, lon = np.arange(128), np.arange(512)
    out = np.zeros((8, 256, 1024), np.float64)
    for b in range(8):
        angle = 2.0 * math.pi * (((8 * a + b)[:, None] * lon[None, :]) % NLON) / NLON
        cos, sin = np.cos(angle), np.sin(angle)
        out[b] = np.block([[cos, sin], [-sin, cos]])
    return out.astype(np.float32)


def grid_kernel(left, table, grid_hbm, slope_hbm, g, out, out_sem):
    for b in range(8):
        if b in (0, 4):
            g[b, :, pl.ds(0, 512)] = jnp.dot(left[b], table[b, :, pl.ds(0, 512)], preferred_element_type=F32)
        else:
            g[b] = jnp.dot(left[b], table[b], preferred_element_type=F32)

    root = math.sqrt(0.5)
    for n, target_hbm in enumerate((grid_hbm, slope_hbm)):

        def combine(i, carry, n=n, target_hbm=target_hbm):
            rows = pl.ds(pl.multiple_of(n * 160 + i * 16, 16), 16)
            for c in range(4):
                re = [g[b, rows, pl.ds(128 * c, 128)] for b in range(8)]
                im = [None if b in (0, 4) else g[b, rows, pl.ds(512 + 128 * c, 128)] for b in range(8)]
                plus, minus = re[0] + re[4], re[0] - re[4]
                r26, i26 = re[2] + re[6], im[6] - im[2]
                even = [plus + r26, minus + i26, plus - r26, minus - i26]
                r17, r35 = re[1] + re[7], re[3] + re[5]
                i71, i53 = im[7] - im[1], im[5] - im[3]
                rr, ii = root * (r17 - r35), root * (i71 + i53)
                odd = [r17 + r35, ii + rr, i71 - i53, ii - rr]
                for j in range(4):
                    out[rows, pl.ds(512 * j + 128 * c, 128)] = (even[j] + odd[j]).astype(BF16)
                    out[rows, pl.ds(512 * j + 2048 + 128 * c, 128)] = (even[j] - odd[j]).astype(BF16)
            pltpu.make_async_copy(out.at[rows], target_hbm.at[pl.ds(pl.multiple_of(i * 16, 16), 16)], out_sem.at[n]).start()
            return carry

        lax.fori_loop(0, 10, combine, 0)
    for n, target_hbm in enumerate((grid_hbm, slope_hbm)):
        pltpu.make_async_copy(out.at[pl.ds(160 * n, 160)], target_hbm, out_sem.at[n]).wait()


def to_grid(left, table):
    vmem = pl.BlockSpec(memory_space=pltpu.VMEM)
    hbm = pl.BlockSpec(memory_space=pltpu.HBM)
    shape = jax.ShapeDtypeStruct((160, NLON), BF16)
    return pl.pallas_call(
        grid_kernel,
        out_shape=(shape, shape),
        in_specs=[vmem, vmem],
        out_specs=(hbm, hbm),
        scratch_shapes=[
            pltpu.VMEM((8, 320, 1024), F32),
            pltpu.VMEM((320, NLON), BF16),
            pltpu.SemaphoreType.DMA((2,)),
        ],
        compiler_params=pltpu.CompilerParams(vmem_limit_bytes=32 << 20),
    )(left, table)


def body(coefficients, section_factors, level_factors, partners, wave_ids):
    y = coefficients.reshape(NW * NF, 2, 2, 4, 128).transpose(0, 2, 3, 1, 4).reshape(NW * NF * 16, 128)
    left = synth(partners, wave_ids, y, section_factors[0], level_factors[0])
    grid, slope = to_grid(left, jnp.asarray(dft_tables(), BF16))
    shape = (2, NF, 8, NLON)
    return (
        grid.reshape(shape).transpose(0, 2, 1, 3),
        slope.reshape(shape).transpose(0, 2, 1, 3),
    )


def solution(mesh):
    in_specs = (
        P("ha", "ma", None, None, None),
        P("ha", "ma", None, None),
        P("ha", None, "ma", None, None),
        P(),
        P(),
    )
    out_specs = (P(None, ("ma", "ha"), None, None), P(None, ("ma", "ha"), None, None))
    return jax.shard_map(body, mesh=mesh, in_specs=in_specs, out_specs=out_specs, check_vma=False)
```

time: 53.5 us -> 32.9 us (0.61)
  Pallas kernels: 45.2 us -> 32.1 us
  local copies, waits for them, and re-layouts: 7.42 us -> 0.01 us
    pallas_call x1, Pallas kernels: 36.6 us -> 29 us  [synth(): pl.pallas_call(synth_kernel, out_shape=jax.ShapeDtypeStruct((8, 320, 256)...]
    unnamed x12 -> x2, local copies, waits for them, and re-layouts: 7.42 us -> 0.01 us
    pallas_call x1, Pallas kernels: 8.58 us -> 3.15 us  [to_grid(): pl.pallas_call(grid_kernel, out_shape=(shape, shape), in_specs=[vmem, vme...]
where the time goes in v2:
time: 32.9 us; the launch traced here: 32.8 us
  Pallas kernels  32.1 us (98%)
  between operations  0.66 us (2%)
    pallas_call x1, Pallas kernels, synth(): pl.pallas_call(synth_kernel, out_shape=jax.ShapeDtypeStruct((8, 320, 256)...  29 us
    pallas_call x1, Pallas kernels, to_grid(): pl.pallas_call(grid_kernel, out_shape=(shape, shape), in_specs=[vmem, vme...  3.15 us

profile of v2, /device:TPU:1, one launch (start us, length us, event | category | flops | bytes accessed | tf_op | source)
XLA Modules:
  0.0 32.8 jit_solution(1408851977060745013)
XLA Ops:
  0.6 0.0 copy-start
  0.6 29.0 %shard_map.77.left = bf16[8,320,256]{2,1,0:T(8,128)(2,1)S(1)} custom-call(s32[2,16]{1,0:T(2,128)} %partners_hbm.1, s32[1024]{0:T(1024)} %waves_hbm.1, s32[8,128]{1,0:T(8,128)} %bitcast.17, bf16[2560,128]{1,0:T(8,128)(2,1)} %bitcast.16, bf16[16,64,1024]{2,1,0:T(8,128)(2,1)} %bitcast.15, bf16[2,16,64,2048]{3,2,1,0:T(8,128)(2,1)} %bitcast.14), custom_call_target="tpu_custom_call" | custom-call | tf_op jit(solution)/shard_map/pallas_call | solution.py:244
  29.6 0.0 copy-done
  29.7 3.1 %shard_map.78 = (bf16[160,4096]{1,0:T(8,128)(2,1)}, bf16[160,4096]{1,0:T(8,128)(2,1)}) custom-call(bf16[8,320,256]{2,1,0:T(8,128)(2,1)S(1)} %shard_map.77.left, bf16[8,256,1024]{2,1,0:T(8,128)(2,1)S(1)} %copy-done), custom_call_target="tpu_custom_call" | custom-call | tf_op jit(solution)/shard_map/pallas_call | solution.py:320
Async XLA Ops:
  0.6 29.0 %copy-start = (bf16[8,256,1024]{2,1,0:T(8,128)(2,1)S(1)}, bf16[8,256,1024]{2,1,0:T(8,128)(2,1)}, u32[]{:S(2)}) copy-start(bf16[8,256,1024]{2,1,0:T(8,128)(2,1)} %constant.2.clone.table) | copy-start | bytes 12582916

commit v3 on v2

--- a/solution.py
+++ b/solution.py
@@ -35,16 +35,20 @@
     return jnp.concatenate([jnp.where(m, block, jnp.zeros_like(block)) for m in masks], axis=0)
 
 
-ORDER = (5, 3, 7, 4, 1, 2, 6, 0)
+ORDER = (7, 3, 5, 1, 6, 2, 4, 0)
 
 
 def pick(bit, base):
     return 1 - base if bit else base
 
 
+def mask_at(step, place):
+    return ORDER[(step + 2 * place) % 8]
+
+
 def synth_kernel(
     partners_hbm, waves_hbm, table_hbm, y_hbm, s_hbm, l_hbm, left,
-    partners, waves, wave_rows, yv, yf, zin, z0, z1, sv, lv, perm, send, recv, acc, in_sem, send_sem, recv_sem, own_sem,
+    partners, waves, wave_rows, yv, yf, zin, z0, z1, sv, lv, perm, send, recv, acc, in_sem, send_sem, recv_sem,
 ):
     ma = lax.axis_index("ma")
     ha = lax.axis_index("ha")
@@ -80,20 +84,20 @@
     lane_wave = (iota((128, 128), 1) % 64) // 10
     masks = [lane_wave == w for w in range(6)]
 
-    yf[pl.ds(2560, 512), :] = jnp.zeros((512, 128), F32)
+    yf[pl.ds(3840, 768), :] = jnp.zeros((768, 128), F32)
     degree = 2 * ((iota((16, 128), 0) // 2) * 128 + iota((16, 128), 1)) + ha
-    greet(0, 16)
+    greet(0, 64)
     loads[1].wait()
     loads[0].wait()
     for w in range(NW):
         keep = degree <= (M - 1) - waves[ma * NW + w]
         for f in range(NF):
             row = (w * NF + f) * 16
-            yf[pl.ds(row, 16), :] = jnp.where(keep, yv[pl.ds(row, 16), :].astype(F32), 0.0)
-        greet(16 + 7 * w, 23 + 7 * w)
+            yf[pl.ds((w * NF + f) * 24, 16), :] = jnp.where(keep, yv[pl.ds(row, 16), :].astype(F32), 0.0)
+        greet(64 + 4 * w, 68 + 4 * w)
     for j in range(8):
         for t in range(3):
-            rows = [yf[pl.ds(t * 960 + 2 * j + part, 64, stride=16), :] for part in range(2)]
+            rows = [yf[pl.ds(t * 1440 + 2 * j + part, 64, stride=24), :] for part in range(2)]
             block = jnp.concatenate(rows, axis=0).astype(BF16)
             turned = lax.dot_general(eye, block, NT, preferred_element_type=F32)
             zin[j, :, pl.ds(t * 128, 128)] = turned.astype(BF16)
@@ -142,17 +146,19 @@
     loads[6].wait()
     pl.semaphore_wait(barrier, 127)
 
-    own = pltpu.make_async_copy(send.at[me], recv.at[slot], own_sem)
     pair = me // 16
     low_bits = [me % 2, (me // 2) % 2, (me // 4) % 2, (me // 8) % 2]
     high = [pair % 2, (pair // 2) % 2, pair // 4]
     half = iota((16, 4, 128), 2) < 64
 
+    at_place = [pick(1 - (n & 1), low_bits[1]) * pick(1 - (n >> 1), low_bits[2]) for n in range(4)]
+
     def partner_pair(mask):
         return sum(pick((mask >> i) & 1, high[i]) * (1 << i) for i in range(3))
 
-    for i, mask in enumerate(ORDER):
-        p = partner_pair(mask)
+    for i in range(8):
+        p = sum(at_place[n] * partner_pair(mask_at(i, n)) for n in range(4))
+        own = p == pair
         blocks = [level(1, 2 * p + k, z1) for k in range(2)]
         state = jnp.concatenate([jnp.concatenate(outs, axis=1) for outs in blocks], axis=0)
         moved = jnp.dot(state, perm[...], preferred_element_type=F32)
@@ -166,35 +172,40 @@
                 send[groups, 4] = jnp.where(half, rows[:, :4], rows[:, 4:]).astype(BF16)
         for r in range(15, -1, -1):
             g = p * 16 + sum(pick((r >> n) & 1, low_bits[n]) * (1 << n) for n in range(4))
-            if mask == 0 and r == 0:
-                own.start()
-            else:
+
+            def go():
                 pltpu.make_async_remote_copy(
                     send.at[g], recv.at[slot], send_sem, recv_sem.at[i], device_id=target(g), device_id_type=MESH
                 ).start()
 
+            if r == 0:
+                pl.when(jnp.logical_not(own))(go)
+                pl.when(own)(pltpu.make_async_copy(send.at[g], recv.at[slot], recv_sem.at[i]).start)
+            else:
+                go()
+
     group = iota((8, 128), 1) // 16
-    for i, mask in enumerate(ORDER):
-        j = partner_pair(mask)
-        slot_wave = wave_rows[pl.ds(j, 1), :]
+    lane_place = (iota((1, 128), 1) // 16) % 4
+    for i in range(8):
+        pairs = [partner_pair(mask_at(i, n)) for n in range(4)]
+        slot_wave = wave_rows[pl.ds(pairs[0], 1), :]
+        for n in range(1, 4):
+            slot_wave = jnp.where(lane_place == n, wave_rows[pl.ds(pairs[n], 1), :], slot_wave)
         row = iota((M, 1), 0)
         k = 8 * (row % 128) + row // 128
         weight = jnp.where(k > 0, 2.0, 1.0)
         onehot = jnp.where(slot_wave == k, weight, 0.0).astype(BF16)
-        count = 16 if mask else 15
         pltpu.make_async_remote_copy(
-            send.at[pl.ds(0, count)], recv.at[pl.ds(0, count)], send_sem, recv_sem.at[i],
+            send.at[pl.ds(0, 16)], recv.at[pl.ds(0, 16)], send_sem, recv_sem.at[i],
             device_id=target(me), device_id_type=MESH,
         ).wait_recv()
-        if mask == 0:
-            own.wait()
         parts = [[None] * 20, [None] * 20]
         for q in range(3):
             sides = []
             for p in range(2):
                 rows = []
                 for n in range(8):
-                    message = recv.at[p * 64 + 8 * j + n]
+                    message = recv.at[p * 64 + 8 * pairs[n % 4] + n]
                     if q < 2:
                         rows.append(jnp.concatenate([message[2 * q].astype(F32), message[2 * q + 1].astype(F32)], axis=0))
                     else:
@@ -251,7 +262,7 @@
             pltpu.SMEM((M,), jnp.int32),
             pltpu.VMEM((8, 128), jnp.int32),
             pltpu.VMEM((2560, 128), BF16),
-            pltpu.VMEM((3072, 128), F32),
+            pltpu.VMEM((4608, 128), F32),
             pltpu.VMEM((8, 128, LANES), BF16),
             pltpu.VMEM((NB, K, LANES), BF16),
             pltpu.VMEM((NB, K, LANES), BF16),
@@ -264,7 +275,6 @@
             pltpu.SemaphoreType.DMA((7,)),
             pltpu.SemaphoreType.DMA,
             pltpu.SemaphoreType.DMA((8,)),
-            pltpu.SemaphoreType.DMA,
         ],
         compiler_params=pltpu.CompilerParams(collective_id=0, has_side_effects=True, vmem_limit_bytes=32 << 20),
     )(*[pltpu.with_memory_space_constraint(v, pltpu.HBM) for v in (partners, waves, waves.reshape(8, 128), y, s, l)])

time: 32.9 us -> 30.4 us (0.924)
  Pallas kernels: 32.1 us -> 29.6 us
    pallas_call x1, Pallas kernels: 29 us -> 26.4 us  [synth(): pl.pallas_call(synth_kernel, out_shape=jax.ShapeDtypeStruct((8, 320, 256)...]
where the time goes in v3:
time: 30.4 us; the launch traced here: 30.2 us
  Pallas kernels  29.6 us (97%)
  between operations  0.66 us (2%)
    pallas_call x1, Pallas kernels, synth(): pl.pallas_call(synth_kernel, out_shape=jax.ShapeDtypeStruct((8, 320, 256)...  26.4 us
    pallas_call x1, Pallas kernels, to_grid(): pl.pallas_call(grid_kernel, out_shape=(shape, shape), in_specs=[vmem, vme...  3.15 us

profile of v3, /device:TPU:1, one launch (start us, length us, event | category | flops | bytes accessed | tf_op | source)
XLA Modules:
  0.0 30.2 jit_solution(15004224810112472290)
XLA Ops:
  0.6 0.0 copy-start
  0.6 26.4 %shard_map.77.left = bf16[8,320,256]{2,1,0:T(8,128)(2,1)S(1)} custom-call(s32[2,16]{1,0:T(2,128)} %partners_hbm.1, s32[1024]{0:T(1024)} %waves_hbm.1, s32[8,128]{1,0:T(8,128)} %bitcast.17, bf16[2560,128]{1,0:T(8,128)(2,1)} %bitcast.16, bf16[16,64,1024]{2,1,0:T(8,128)(2,1)} %bitcast.15, bf16[2,16,64,2048]{3,2,1,0:T(8,128)(2,1)} %bitcast.14), custom_call_target="tpu_custom_call" | custom-call | tf_op jit(solution)/shard_map/pallas_call | solution.py:255
  27.1 0.0 copy-done
  27.1 3.1 %shard_map.78 = (bf16[160,4096]{1,0:T(8,128)(2,1)}, bf16[160,4096]{1,0:T(8,128)(2,1)}) custom-call(bf16[8,320,256]{2,1,0:T(8,128)(2,1)S(1)} %shard_map.77.left, bf16[8,256,1024]{2,1,0:T(8,128)(2,1)S(1)} %copy-done), custom_call_target="tpu_custom_call" | custom-call | tf_op jit(solution)/shard_map/pallas_call | solution.py:330
Async XLA Ops:
  0.6 26.5 %copy-start = (bf16[8,256,1024]{2,1,0:T(8,128)(2,1)S(1)}, bf16[8,256,1024]{2,1,0:T(8,128)(2,1)}, u32[]{:S(2)}) copy-start(bf16[8,256,1024]{2,1,0:T(8,128)(2,1)} %constant.2.clone.table) | copy-start | bytes 12582916

commit v4 on v3

--- a/solution.py
+++ b/solution.py
@@ -48,7 +48,7 @@
 
 def synth_kernel(
     partners_hbm, waves_hbm, table_hbm, y_hbm, s_hbm, l_hbm, left,
-    partners, waves, wave_rows, yv, yf, zin, z0, z1, sv, lv, perm, send, recv, acc, in_sem, send_sem, recv_sem,
+    partners, waves, wave_rows, yv, yf, zin, z0, z1, sv, lv, perm, send, recv, onehot, acc, in_sem, send_sem, recv_sem,
 ):
     ma = lax.axis_index("ma")
     ha = lax.axis_index("ha")
@@ -62,10 +62,23 @@
         pltpu.make_async_copy(table_hbm, wave_rows, in_sem.at[3]),
         pltpu.make_async_copy(s_hbm, sv, in_sem.at[4]),
         pltpu.make_async_copy(l_hbm.at[0], lv.at[0], in_sem.at[5]),
-        pltpu.make_async_copy(l_hbm.at[1], lv.at[1], in_sem.at[6]),
     ]
-    for load in loads[:6]:
+    for load in loads:
         load.start()
+
+    pair = me // 16
+    low_bits = [me % 2, (me // 2) % 2, (me // 4) % 2, (me // 8) % 2]
+    high = [pair % 2, (pair // 2) % 2, pair // 4]
+    at_place = [pick(1 - (n & 1), low_bits[1]) * pick(1 - (n >> 1), low_bits[2]) for n in range(4)]
+
+    def partner_pair(mask):
+        return sum(pick((mask >> i) & 1, high[i]) * (1 << i) for i in range(3))
+
+    order = [sum(at_place[n] * partner_pair(mask_at(i, n)) for n in range(4)) for i in range(8)]
+    late_loads = []
+    for i, p in enumerate(order):
+        lanes = pl.ds(pl.multiple_of(p * 256, 256), 256)
+        late_loads.append(pltpu.make_async_copy(l_hbm.at[1, :, :, lanes], lv.at[1, :, :, lanes], in_sem.at[6 + i]))
 
     barrier = pltpu.get_barrier_semaphore()
 
@@ -103,52 +116,44 @@
             zin[j, :, pl.ds(t * 128, 128)] = turned.astype(BF16)
 
     loads[4].wait()
-    loads[6].start()
-    low = iota((64, 128), 1) < 64
+    for load in late_loads:
+        load.start()
+    half_masks = [m[:64] for m in masks]
 
     def section(j, carry):
         lanes = pl.ds(pl.multiple_of(j * 128, 128), 128)
         for t, (first, last) in enumerate(TILE_WAVES):
-            halves = []
-            for w in range(first, last):
-                factor = sv[w, :, lanes]
-                zero = jnp.zeros_like(factor)
-                halves.append(jnp.concatenate([jnp.where(low, factor, zero), jnp.where(low, zero, factor)], axis=0))
-            right = keep_waves(zin[j, :, pl.ds(t * 128, 128)], masks[: last - first])
-            out = jnp.dot(jnp.concatenate(halves, axis=1), right, preferred_element_type=F32).astype(BF16)
-            z0[2 * j, :, pl.ds(t * 128, 128)] = out[:64]
-            z0[2 * j + 1, :, pl.ds(t * 128, 128)] = out[64:]
+            for k in range(2):
+                side = slice(64 * k, 64 * k + 64)
+                factors = jnp.concatenate([sv[w, :, lanes][:, side] for w in range(first, last)], axis=1)
+                right = keep_waves(zin[j, pl.ds(64 * k, 64), pl.ds(t * 128, 128)], half_masks[: last - first])
+                out = jnp.dot(factors, right, preferred_element_type=F32)
+                z0[2 * j + k, :, pl.ds(t * 128, 128)] = out.astype(BF16)
         return carry
 
     lax.fori_loop(0, 8, section, 0, unroll=2)
 
-    def level(l, b, z):
-        other = partners[l, b]
+    def level(l, b, own_state, other_state):
         lanes = pl.ds(pl.multiple_of(b * 128, 128), 128)
         outs = []
         for t, (first, last) in enumerate(TILE_WAVES):
             factors = jnp.concatenate([lv[l, w, :, lanes] for w in range(first, last)], axis=1)
-            both = jnp.concatenate([z[b, :, pl.ds(t * 128, 128)], z[other, :, pl.ds(t * 128, 128)]], axis=0)
-            right = keep_waves(both, masks[: last - first])
+            right = keep_waves(jnp.concatenate([own_state[t], other_state[t]], axis=0), masks[: last - first])
             outs.append(jnp.dot(factors, right, preferred_element_type=F32).astype(BF16))
         return outs
+
+    def tiles(z, b):
+        return [z[b, :, pl.ds(t * 128, 128)] for t in range(3)]
+
+    def first_level(b, carry):
+        for t, out in enumerate(level(0, b, tiles(z0, b), tiles(z0, partners[0, b]))):
+            z1[b, :, pl.ds(t * 128, 128)] = out
+        return carry
 
     loads[2].wait()
     loads[3].wait()
     loads[5].wait()
-
-    def first_level(b, carry):
-        for t, out in enumerate(level(0, b, z0)):
-            z1[b, :, pl.ds(t * 128, 128)] = out
-        return carry
-
-    lax.fori_loop(0, NB, first_level, 0, unroll=4)
-    loads[6].wait()
-    pl.semaphore_wait(barrier, 127)
-
-    pair = me // 16
-    low_bits = [me % 2, (me // 2) % 2, (me // 4) % 2, (me // 8) % 2]
-    high = [pair % 2, (pair // 2) % 2, pair // 4]
+    lax.fori_loop(0, NB, first_level, 0, unroll=8)
     half = iota((16, 4, 128), 2) < 64
 
     at_place = [pick(1 - (n & 1), low_bits[1]) * pick(1 - (n >> 1), low_bits[2]) for n in range(4)]
@@ -156,10 +161,12 @@
     def partner_pair(mask):
         return sum(pick((mask >> i) & 1, high[i]) * (1 << i) for i in range(3))
 
-    for i in range(8):
-        p = sum(at_place[n] * partner_pair(mask_at(i, n)) for n in range(4))
+    for i, p in enumerate(order):
         own = p == pair
-        blocks = [level(1, 2 * p + k, z1) for k in range(2)]
+        late_loads[i].wait()
+        blocks = [level(1, 2 * p + k, tiles(z1, 2 * p + k), tiles(z1, partners[1, 2 * p + k])) for k in range(2)]
+        if i == 0:
+            pl.semaphore_wait(barrier, 127)
         state = jnp.concatenate([jnp.concatenate(outs, axis=1) for outs in blocks], axis=0)
         moved = jnp.dot(state, perm[...], preferred_element_type=F32)
         groups = pl.ds(p * 16, 16)
@@ -186,15 +193,18 @@
 
     group = iota((8, 128), 1) // 16
     lane_place = (iota((1, 128), 1) // 16) % 4
+    row = iota((M, 1), 0)
+    k = 8 * (row % 128) + row // 128
+    weight = jnp.where(k > 0, 2.0, 1.0)
     for i in range(8):
         pairs = [partner_pair(mask_at(i, n)) for n in range(4)]
         slot_wave = wave_rows[pl.ds(pairs[0], 1), :]
         for n in range(1, 4):
             slot_wave = jnp.where(lane_place == n, wave_rows[pl.ds(pairs[n], 1), :], slot_wave)
-        row = iota((M, 1), 0)
-        k = 8 * (row % 128) + row // 128
-        weight = jnp.where(k > 0, 2.0, 1.0)
-        onehot = jnp.where(slot_wave == k, weight, 0.0).astype(BF16)
+        onehot[i] = jnp.where(slot_wave == k, weight, 0.0).astype(BF16)
+
+    for i in range(8):
+        pairs = [partner_pair(mask_at(i, n)) for n in range(4)]
         pltpu.make_async_remote_copy(
             send.at[pl.ds(0, 16)], recv.at[pl.ds(0, 16)], send_sem, recv_sem.at[i],
             device_id=target(me), device_id_type=MESH,
@@ -232,7 +242,7 @@
         spectra = jnp.concatenate(parts[0] + parts[1], axis=0).astype(BF16)
         for b in range(8):
             lanes = pl.ds(b * 128, 128)
-            moved = lax.dot_general(spectra, onehot[b * 128 : (b + 1) * 128], NT, preferred_element_type=F32)
+            moved = lax.dot_general(spectra, onehot[i, pl.ds(b * 128, 128), :], NT, preferred_element_type=F32)
             if i > 0:
                 moved = moved + acc[:, lanes]
             if i < 7:
@@ -271,8 +281,9 @@
             pltpu.VMEM((LANES, LANES), BF16),
             pltpu.VMEM((128, 5, 4, 128), BF16),
             pltpu.VMEM((128, 5, 4, 128), BF16),
+            pltpu.VMEM((8, M, 128), BF16),
             pltpu.VMEM((320, M), F32),
-            pltpu.SemaphoreType.DMA((7,)),
+            pltpu.SemaphoreType.DMA((14,)),
             pltpu.SemaphoreType.DMA,
             pltpu.SemaphoreType.DMA((8,)),
         ],
@@ -318,7 +329,7 @@
             pltpu.make_async_copy(out.at[rows], target_hbm.at[pl.ds(pl.multiple_of(i * 16, 16), 16)], out_sem.at[n]).start()
             return carry
 
-        lax.fori_loop(0, 10, combine, 0)
+        lax.fori_loop(0, 10, combine, 0, unroll=2)
     for n, target_hbm in enumerate((grid_hbm, slope_hbm)):
         pltpu.make_async_copy(out.at[pl.ds(160 * n, 160)], target_hbm, out_sem.at[n]).wait()
 

time: 30.4 us -> 29.9 us (0.984)
  Pallas kernels: 29.6 us -> 29.1 us
where the time goes in v4:
time: 29.9 us; the launch traced here: 29.8 us
  Pallas kernels  29.1 us (97%)
  between operations  0.66 us (2%)
    pallas_call x1, Pallas kernels, synth(): pl.pallas_call(synth_kernel, out_shape=jax.ShapeDtypeStruct((8, 320, 256)...  26.1 us
    pallas_call x1, Pallas kernels, to_grid(): pl.pallas_call(grid_kernel, out_shape=(shape, shape), in_specs=[vmem, vme...  3 us

profile of v4, /device:TPU:1, one launch (start us, length us, event | category | flops | bytes accessed | tf_op | source)
XLA Modules:
  0.0 29.8 jit_solution(845856067420075872)
XLA Ops:
  0.6 0.0 copy-start
  0.6 26.1 %shard_map.77.left = bf16[8,320,256]{2,1,0:T(8,128)(2,1)S(1)} custom-call(s32[2,16]{1,0:T(2,128)} %partners_hbm.1, s32[1024]{0:T(1024)} %waves_hbm.1, s32[8,128]{1,0:T(8,128)} %bitcast.17, bf16[2560,128]{1,0:T(8,128)(2,1)} %bitcast.16, bf16[16,64,1024]{2,1,0:T(8,128)(2,1)} %bitcast.15, bf16[2,16,64,2048]{3,2,1,0:T(8,128)(2,1)} %bitcast.14), custom_call_target="tpu_custom_call" | custom-call | tf_op jit(solution)/shard_map/pallas_call | solution.py:265
  26.8 0.0 copy-done
  26.8 3.0 %shard_map.78 = (bf16[160,4096]{1,0:T(8,128)(2,1)}, bf16[160,4096]{1,0:T(8,128)(2,1)}) custom-call(bf16[8,320,256]{2,1,0:T(8,128)(2,1)S(1)} %shard_map.77.left, bf16[8,256,1024]{2,1,0:T(8,128)(2,1)S(1)} %copy-done), custom_call_target="tpu_custom_call" | custom-call | tf_op jit(solution)/shard_map/pallas_call | solution.py:341
Async XLA Ops:
  0.6 26.2 %copy-start = (bf16[8,256,1024]{2,1,0:T(8,128)(2,1)S(1)}, bf16[8,256,1024]{2,1,0:T(8,128)(2,1)}, u32[]{:S(2)}) copy-start(bf16[8,256,1024]{2,1,0:T(8,128)(2,1)} %constant.2.clone.table) | copy-start | bytes 12582916

commit v5 on v4

--- a/solution.py
+++ b/solution.py
@@ -43,7 +43,7 @@
 
 
 def mask_at(step, place):
-    return ORDER[(step + 2 * place) % 8]
+    return ORDER[(step + (0, 4, 1, 5)[place]) % 8]
 
 
 def synth_kernel(
@@ -177,7 +177,7 @@
                 send[groups, 2 * t + 1] = rows[:, 4:].astype(BF16)
             else:
                 send[groups, 4] = jnp.where(half, rows[:, :4], rows[:, 4:]).astype(BF16)
-        for r in range(15, -1, -1):
+        for r in (9, 1, 11, 3, 13, 5, 15, 7, 8, 10, 2, 12, 4, 14, 6, 0):
             g = p * 16 + sum(pick((r >> n) & 1, low_bits[n]) * (1 << n) for n in range(4))
 
             def go():
@@ -329,7 +329,7 @@
             pltpu.make_async_copy(out.at[rows], target_hbm.at[pl.ds(pl.multiple_of(i * 16, 16), 16)], out_sem.at[n]).start()
             return carry
 
-        lax.fori_loop(0, 10, combine, 0, unroll=2)
+        lax.fori_loop(0, 10, combine, 0, unroll=5)
     for n, target_hbm in enumerate((grid_hbm, slope_hbm)):
         pltpu.make_async_copy(out.at[pl.ds(160 * n, 160)], target_hbm, out_sem.at[n]).wait()
 

time: 29.9 us -> 29.8 us (level)
  no operation moved by 1% of the time
where the time goes in v5:
time: 29.8 us; the launch traced here: 29.7 us
  Pallas kernels  29 us (97%)
  between operations  0.66 us (2%)
    pallas_call x1, Pallas kernels, synth(): pl.pallas_call(synth_kernel, out_shape=jax.ShapeDtypeStruct((8, 320, 256)...  26.1 us
    pallas_call x1, Pallas kernels, to_grid(): pl.pallas_call(grid_kernel, out_shape=(shape, shape), in_specs=[vmem, vme...  2.92 us

profile of v5, /device:TPU:1, one launch (start us, length us, event | category | flops | bytes accessed | tf_op | source)
XLA Modules:
  0.0 29.7 jit_solution(16405337373875446122)
XLA Ops:
  0.6 0.0 copy-start
  0.6 26.1 %shard_map.77.left = bf16[8,320,256]{2,1,0:T(8,128)(2,1)S(1)} custom-call(s32[2,16]{1,0:T(2,128)} %partners_hbm.1, s32[1024]{0:T(1024)} %waves_hbm.1, s32[8,128]{1,0:T(8,128)} %bitcast.17, bf16[2560,128]{1,0:T(8,128)(2,1)} %bitcast.16, bf16[16,64,1024]{2,1,0:T(8,128)(2,1)} %bitcast.15, bf16[2,16,64,2048]{3,2,1,0:T(8,128)(2,1)} %bitcast.14), custom_call_target="tpu_custom_call" | custom-call | tf_op jit(solution)/shard_map/pallas_call | solution.py:265
  26.8 0.0 copy-done
  26.8 2.9 %shard_map.78 = (bf16[160,4096]{1,0:T(8,128)(2,1)}, bf16[160,4096]{1,0:T(8,128)(2,1)}) custom-call(bf16[8,320,256]{2,1,0:T(8,128)(2,1)S(1)} %shard_map.77.left, bf16[8,256,1024]{2,1,0:T(8,128)(2,1)S(1)} %copy-done), custom_call_target="tpu_custom_call" | custom-call | tf_op jit(solution)/shard_map/pallas_call | solution.py:341
Async XLA Ops:
  0.6 26.1 %copy-start = (bf16[8,256,1024]{2,1,0:T(8,128)(2,1)S(1)}, bf16[8,256,1024]{2,1,0:T(8,128)(2,1)}, u32[]{:S(2)}) copy-start(bf16[8,256,1024]{2,1,0:T(8,128)(2,1)} %constant.2.clone.table) | copy-start | bytes 12582916
